TPU v7x, 128 devices: a whole 4x4x4 slice. The times are simulated.
128 devices in a mesh: expert: 16 (over x, y), tensor: 8 (over z, core).
Axes of the slice: x: 4, y: 4, z: 4, core: 2. Of those that a mesh axis runs over, the one named last changes fastest.
Arguments:
- tokens: bfloat16 [2048, 7168], P('expert', 'tensor'), may hold values from -6 to 6
- cotangent: bfloat16 [2048, 7168], P('expert', 'tensor'), may hold values from -6 to 6
- routes: int32 [2048, 2], P('expert'), may hold values from 0 to 15, all different within a row; in each aligned block of 128 rows (0 to 127, 128 to 255, ...) at most 32 rows name the same one
- route_weights: bfloat16 [2048, 2], P('expert'), may hold values from 0.099609375 to 1
- capacity_plan: int32 [16], replicated, may hold values from 1 to 32, as said below
- up_weight: bfloat16 [16, 7168, 2432], P('expert', 'tensor'), may hold values from -0.0625 to 0.0625
- down_weight: bfloat16 [16, 2432, 7168], P('expert', None, 'tensor'), may hold values from -0.125 to 0.125
Outputs:
- layer_out: bfloat16 [2048, 7168], P('expert', 'tensor')
- token_grad: bfloat16 [2048, 7168], P('expert', 'tensor')
- up_grad: bfloat16 [16, 7168, 2432], P('expert', 'tensor')
- down_grad: bfloat16 [16, 2432, 7168], P('expert', None, 'tensor')
Inputs may be any that keep to these rules, and one draw needn't show every extreme that they name: `routes`: within each aligned block of 128 tokens no expert is named more than 32 times, and a token's two experts differ. `capacity_plan`: some expert has exactly 32 and some exactly 1.
All inputs are finite; a program needn't handle non-finite values.
Results may differ from a plain program's by a relative error of at most 0.0063.
Values may be sent and summed in bfloat16 or wider, within the bound.
A program may use at most 128 MiB of HBM per device.

v0:
```python
import jax
import jax.numpy as jnp
from jax import lax
from jax.sharding import PartitionSpec as P


def slot_layout(routes, capacity_plan, experts, capacity):
    pair_ids = routes.reshape(-1)
    onehot = (pair_ids[:, None] == jnp.arange(experts, dtype=jnp.int32)[None, :]).astype(jnp.int32)
    earlier = jnp.cumsum(onehot, axis=0) - onehot
    position = jnp.sum(earlier * onehot, axis=1)
    limits = jnp.sum(onehot * capacity_plan[None, :], axis=1)
    kept_mask = position < limits
    slot_ids = jnp.where(kept_mask, pair_ids * capacity + position, experts * capacity)
    return (slot_ids.reshape(routes.shape), kept_mask.reshape(routes.shape))


def contract_last(left, right):
    return lax.dot_general(
        left, right, (((1,), (1,)), ((), ())), preferred_element_type=jnp.float32
    )


def contract_first(left, right):
    return lax.dot_general(
        left, right, (((0,), (0,)), ((), ())), preferred_element_type=jnp.float32
    )


def per_device(tokens, cotangent, routes, route_weights, capacity_plan, up_weight, down_weight):
    experts = lax.axis_size("expert")
    tok_rows, features = tokens.shape
    capacity = 4 * tok_rows // experts
    slot_ids, kept_mask = slot_layout(routes, capacity_plan, experts, capacity)
    matches = slot_ids[:, :, None] == jnp.arange(experts * capacity, dtype=jnp.int32)[None, None, :]
    placer = jnp.any(matches, axis=1).T.astype(jnp.bfloat16)
    weight_terms = jnp.where(matches, route_weights[:, :, None].astype(jnp.float32), 0.0)
    slot_weight = jnp.sum(weight_terms, axis=(0, 1)).astype(jnp.bfloat16).reshape(experts, capacity)
    sent_rows = jnp.dot(placer, tokens, preferred_element_type=jnp.float32).astype(jnp.bfloat16)
    sent_grads = jnp.dot(placer, cotangent, preferred_element_type=jnp.float32).astype(jnp.bfloat16)
    received = (
        lax.all_to_all(
            sent_rows.reshape(experts, capacity, features),
            "expert",
            split_axis=0,
            concat_axis=0,
            tiled=True,
        ),
        lax.all_to_all(
            sent_grads.reshape(experts, capacity, features),
            "expert",
            split_axis=0,
            concat_axis=0,
            tiled=True,
        ),
        lax.all_to_all(slot_weight, "expert", split_axis=0, concat_axis=0, tiled=True),
    )
    expert_rows = received[0].reshape(-1, features)
    rows_dy = received[1].reshape(-1, features)
    rows_weight = received[2].reshape(-1)
    up_local = up_weight[0]
    down_local = down_weight[0]
    grad_rows = (rows_weight.astype(jnp.float32)[:, None] * rows_dy.astype(jnp.float32)).astype(
        jnp.bfloat16
    )
    pre_act = lax.psum(jnp.dot(expert_rows, up_local, preferred_element_type=jnp.float32), "tensor")
    gate_sig = jax.nn.sigmoid(pre_act)
    hidden = (pre_act * gate_sig).astype(jnp.bfloat16)
    d_hidden = lax.psum(contract_last(grad_rows, down_local), "tensor")
    slope = (d_hidden * gate_sig * (1.0 + pre_act * (1.0 - gate_sig))).astype(jnp.bfloat16)
    expert_out = jnp.dot(hidden, down_local, preferred_element_type=jnp.float32).astype(
        jnp.bfloat16
    )
    returned = lax.all_to_all(
        expert_out.reshape(experts, capacity, features),
        "expert",
        split_axis=0,
        concat_axis=0,
        tiled=True,
    )
    down_grad = contract_first(hidden, grad_rows).astype(jnp.bfloat16)[None]
    up_grad = contract_first(expert_rows, slope).astype(jnp.bfloat16)[None]
    row_grad = contract_last(slope, up_local).astype(jnp.bfloat16)
    returned_grad = lax.all_to_all(
        row_grad.reshape(experts, capacity, features),
        "expert",
        split_axis=0,
        concat_axis=0,
        tiled=True,
    )
    spare = jnp.zeros((1, features), jnp.bfloat16)
    kept_float = kept_mask.astype(jnp.float32)
    scale = kept_float * route_weights.astype(jnp.float32)
    out_flat = jnp.concatenate([returned.reshape(-1, features), spare], axis=0)
    picked = out_flat[slot_ids].astype(jnp.float32)
    layer_out = jnp.sum(scale[:, :, None] * picked, axis=1).astype(jnp.bfloat16)
    grad_flat = jnp.concatenate([returned_grad.reshape(-1, features), spare], axis=0)
    picked_grad = grad_flat[slot_ids].astype(jnp.float32)
    token_grad = jnp.sum(kept_float[:, :, None] * picked_grad, axis=1).astype(jnp.bfloat16)
    return (layer_out, token_grad, up_grad, down_grad)


def solution(mesh):
    placed = (
        P("expert", "tensor"),
        P("expert", "tensor"),
        P("expert", None),
        P("expert", None),
        P(),
        P("expert", "tensor", None),
        P("expert", None, "tensor"),
    )
    return jax.shard_map(
        per_device,
        mesh=mesh,
        in_specs=placed,
        out_specs=(
            P("expert", "tensor"),
            P("expert", "tensor"),
            P("expert", "tensor", None),
            P("expert", None, "tensor"),
        ),
        check_vma=False,
    )
```

profile of v0, /device:TPU:1, one launch (start us, length us, event | category | flops | bytes accessed | tf_op | source)
XLA Modules:
  0.0 253.2 jit_solution(11388003207178205124)
XLA Ops:
  7.2 0.8 copy.45
  8.3 0.6 reduce-window.6
  9.1 0.8 select_reduce_fusion.1
  10.3 0.7 compare_select_fusion
  11.0 0.7 convert_element_type.105
  11.8 0.7 convert_element_type.136
  12.5 7.6 %all-to-all-start.2 = ((bf16[16,1,32]{2,1,0:T(2,128)(2,1)}), bf16[16,1,32]{2,1,0:T(2,128)(2,1)S(1)}, u32[]{:S(2)}, u32[]{:S(2)}) async-start(bf16[16,1,32]{2,1,0:T(2,128)(2,1)} %convert_element_type.136), calls=%async_computation.2 | async-start | bytes 16384 | tf_op jit(solution)/shard_map/all_to_all | solution.py:56
  20.2 1.4 convolution_convert_fusion.2
  21.6 4.8 %all-to-all-done.2 = bf16[16,1,32]{2,1,0:T(2,128)(2,1)S(1)} async-done(((bf16[16,1,32]{2,1,0:T(2,128)(2,1)}), bf16[16,1,32]{2,1,0:T(2,128)(2,1)S(1)}, u32[]{:S(2)}, u32[]{:S(2)}) %all-to-all-start.2) | async-done | bytes 1056 | tf_op jit(solution)/shard_map/all_to_all | solution.py:56
  26.4 3.6 %all-to-all-start.3 = ((bf16[16,32,896]{2,1,0:T(8,128)(2,1)}), bf16[16,32,896]{2,1,0:T(8,128)(2,1)S(1)}, u32[]{:S(2)}, u32[]{:S(2)}) async-start(bf16[16,32,896]{2,1,0:T(8,128)(2,1)} %bitcast.8), calls=%async_computation.3 | async-start | bytes 1835008 | tf_op jit(solution)/shard_map/all_to_all | solution.py:49
  30.1 2.3 convolution_convert_fusion.3
  32.4 11.1 %all-to-all-done.3 = bf16[16,32,896]{2,1,0:T(8,128)(2,1)S(1)} async-done(((bf16[16,32,896]{2,1,0:T(8,128)(2,1)}), bf16[16,32,896]{2,1,0:T(8,128)(2,1)S(1)}, u32[]{:S(2)}, u32[]{:S(2)}) %all-to-all-start.3) | async-done | bytes 917536 | tf_op jit(solution)/shard_map/all_to_all | solution.py:49
  43.5 4.4 %all-to-all-start = ((bf16[16,32,896]{2,1,0:T(8,128)(2,1)}), bf16[16,32,896]{2,1,0:T(8,128)(2,1)S(1)}, u32[]{:S(2)}, u32[]{:S(2)}) async-start(bf16[16,32,896]{2,1,0:T(8,128)(2,1)} %bitcast.1), calls=%async_computation | async-start | bytes 1835008 | tf_op jit(solution)/shard_map/all_to_all | solution.py:42
  48.2 6.8 %fusion.2 = f32[512,2432]{1,0:T(8,128)} fusion(bf16[512,896]{1,0:T(8,128)(2,1)S(1)} %bitcast.64, bf16[1,2432,896]{2,1,0:T(8,128)(2,1)} %param.13), kind=kOutput, calls=%fused_computation.9 | convolution fusion | flops 2231369728 | bytes 10256384 | tf_op jit(solution)/shard_map/dot_general | solution.py:19
  55.0 6.1 %all-to-all-done = bf16[16,32,896]{2,1,0:T(8,128)(2,1)S(1)} async-done(((bf16[16,32,896]{2,1,0:T(8,128)(2,1)}), bf16[16,32,896]{2,1,0:T(8,128)(2,1)S(1)}, u32[]{:S(2)}, u32[]{:S(2)}) %all-to-all-start) | async-done | bytes 917536 | tf_op jit(solution)/shard_map/all_to_all | solution.py:42
  61.2 6.7 %fusion.8 = f32[512,2432]{1,0:T(8,128)} fusion(bf16[512,896]{1,0:T(8,128)(2,1)S(1)} %bitcast.62, bf16[1,896,2432]{2,1,0:T(8,128)(2,1)} %param.12), kind=kOutput, calls=%fused_computation.15 | convolution fusion | flops 2231369728 | bytes 10256384 | tf_op jit(solution)/shard_map/dot_general | solution.py:66
  68.7 0.7 copy.53
  69.5 1.1 fusion.10
  70.7 117.9 %all-reduce.5.cloned.1.call-done = (f32[512,2432]{1,0:T(8,128)}, f32[512,2432]{1,0:T(8,128)}) async-done(((f32[512,2432]{1,0:T(8,128)}, f32[512,2432]{1,0:T(8,128)}), (f32[512,2432]{1,0:T(8,128)}, f32[512,2432]{1,0:T(8,128)})) %all-reduce.5.cloned.1.call-update) | async-done | bytes 9961488 | tf_op jit(solution)/shard_map/psum | solution.py:66
  188.6 4.8 %multiply_convert_fusion = bf16[512,2432]{1,0:T(8,128)(2,1)S(1)} fusion(f32[512,2432]{1,0:T(8,128)} %get-tuple-element.6, f32[512,2432]{1,0:T(8,128)} %get-tuple-element.7), kind=kLoop, calls=%fused_computation.4 | loop fusion | flops 11206656 | bytes 12451840 | tf_op jit(solution)/shard_map/convert_element_type | solution.py:70
  193.4 6.0 %fusion.11 = bf16[512,896]{1,0:T(8,128)(2,1)} fusion(bf16[512,2432]{1,0:T(8,128)(2,1)S(1)} %multiply_convert_fusion, bf16[1,896,2432]{2,1,0:T(8,128)(2,1)} %param.12), kind=kOutput, calls=%fused_computation.20 | convolution fusion | flops 2231828480 | bytes 7766016 | tf_op jit(solution)/shard_map/dot_general | solution.py:19
  199.4 4.7 %fusion = bf16[1,896,2432]{2,1,0:T(8,128)(2,1)} fusion(bf16[512,896]{1,0:T(8,128)(2,1)S(1)} %bitcast.63, bf16[512,2432]{1,0:T(8,128)(2,1)S(1)} %multiply_convert_fusion), kind=kOutput, calls=%fused_computation.7 | convolution fusion | flops 2233548800 | bytes 7766016 | tf_op jit(solution)/shard_map/dot_general | solution.py:25
  204.1 6.5 %all-to-all-start.4 = ((bf16[16,32,896]{2,1,0:T(8,128)(2,1)}), bf16[16,32,896]{2,1,0:T(8,128)(2,1)S(1)}, u32[]{:S(2)}, u32[]{:S(2)}) async-start(bf16[16,32,896]{2,1,0:T(8,128)(2,1)} %bitcast.10), calls=%async_computation.4 | async-start | bytes 1835008 | tf_op jit(solution)/shard_map/all_to_all | solution.py:84
  210.7 7.6 %fusion.14 = bf16[512,896]{1,0:T(8,128)(2,1)} fusion(bf16[1,2432,896]{2,1,0:T(8,128)(2,1)} %param.13, f32[512,2432]{1,0:T(8,128)} %get-tuple-element.6), kind=kOutput, calls=%fused_computation.21 | convolution fusion | flops 2238054400 | bytes 10256384 | tf_op jit(solution)/shard_map/dot_general | solution.py:71
  218.2 6.3 %all-to-all-done.4 = bf16[16,32,896]{2,1,0:T(8,128)(2,1)S(1)} async-done(((bf16[16,32,896]{2,1,0:T(8,128)(2,1)}), bf16[16,32,896]{2,1,0:T(8,128)(2,1)S(1)}, u32[]{:S(2)}, u32[]{:S(2)}) %all-to-all-start.4) | async-done | bytes 917536 | tf_op jit(solution)/shard_map/all_to_all | solution.py:84
  224.5 3.9 %all-to-all-start.1 = ((bf16[16,32,896]{2,1,0:T(8,128)(2,1)}), bf16[16,32,896]{2,1,0:T(8,128)(2,1)S(1)}, u32[]{:S(2)}, u32[]{:S(2)}) async-start(bf16[16,32,896]{2,1,0:T(8,128)(2,1)} %bitcast.5), calls=%async_computation.1 | async-start | bytes 1835008 | tf_op jit(solution)/shard_map/all_to_all | solution.py:74
  228.4 7.4 %fusion.1 = bf16[1,2432,896]{2,1,0:T(8,128)(2,1)} fusion(bf16[512,896]{1,0:T(8,128)(2,1)S(1)} %copy-done.1, f32[512,2432]{1,0:T(8,128)} %get-tuple-element.6), kind=kOutput, calls=%fused_computation.8 | convolution fusion | flops 2239774720 | bytes 10256384 | tf_op jit(solution)/shard_map/dot_general | solution.py:25
  235.9 1.2 gather_fusion.1
  237.1 0.5 reshape.143
  237.6 4.0 %all-to-all-done.1 = bf16[16,32,896]{2,1,0:T(8,128)(2,1)S(1)} async-done(((bf16[16,32,896]{2,1,0:T(8,128)(2,1)}), bf16[16,32,896]{2,1,0:T(8,128)(2,1)S(1)}, u32[]{:S(2)}, u32[]{:S(2)}) %all-to-all-start.1) | async-done | bytes 917536 | tf_op jit(solution)/shard_map/all_to_all | solution.py:74
  241.6 1.2 gather_fusion
  243.3 3.0 %multiply_reduce_fusion = (bf16[128,896]{1,0:T(8,128)(2,1)}, bf16[128,896]{1,0:T(8,128)(2,1)}) fusion(f32[128,2,896]{2,1,0:T(2,128)S(1)} %reshape.143, f32[128,2]{1,0:T(8,128)S(1)} %copy-done.2, f32[128,2,896]{2,1,0:T(2,128)S(1)} %reshape.142, f32[128,2]{1,0:T(8,128)S(1)} %copy.50), kind=kLoop, calls=%fused_computation.24 | loop fusion | flops 688128 | bytes 2295808 | tf_op jit(solution)/shard_map/reduce_sum | solution.py:99
  (35 shorter events, 3.0 us)
Async XLA Ops:
  7.2 13.1 %copy-start = (bf16[128,896]{1,0:T(8,128)(2,1)S(1)}, bf16[128,896]{1,0:T(8,128)(2,1)}, u32[]{:S(2)}) copy-start(bf16[128,896]{1,0:T(8,128)(2,1)} %param.8) | copy-start | bytes 688132
  12.5 13.9 %all-to-all-start.2 = ((bf16[16,1,32]{2,1,0:T(2,128)(2,1)}), bf16[16,1,32]{2,1,0:T(2,128)(2,1)S(1)}, u32[]{:S(2)}, u32[]{:S(2)}) async-start(bf16[16,1,32]{2,1,0:T(2,128)(2,1)} %convert_element_type.136), calls=%async_computation.2 | async-start | bytes 16384 | tf_op jit(solution)/shard_map/all_to_all | solution.py:56
  26.4 17.1 %all-to-all-start.3 = ((bf16[16,32,896]{2,1,0:T(8,128)(2,1)}), bf16[16,32,896]{2,1,0:T(8,128)(2,1)S(1)}, u32[]{:S(2)}, u32[]{:S(2)}) async-start(bf16[16,32,896]{2,1,0:T(8,128)(2,1)} %bitcast.8), calls=%async_computation.3 | async-start | bytes 1835008 | tf_op jit(solution)/shard_map/all_to_all | solution.py:49
  43.5 17.6 %all-to-all-start = ((bf16[16,32,896]{2,1,0:T(8,128)(2,1)}), bf16[16,32,896]{2,1,0:T(8,128)(2,1)S(1)}, u32[]{:S(2)}, u32[]{:S(2)}) async-start(bf16[16,32,896]{2,1,0:T(8,128)(2,1)} %bitcast.1), calls=%async_computation | async-start | bytes 1835008 | tf_op jit(solution)/shard_map/all_to_all | solution.py:42
  47.9 140.7 %all-reduce.5.cloned.1.call-start = ((), (), s32[]{:S(2)}) async-start(), calls=%async_computation.5 | async-start | bytes 19922944 | tf_op jit(solution)/shard_map/psum | solution.py:66
  67.9 0.7 copy-start.3
  204.1 20.4 %all-to-all-start.4 = ((bf16[16,32,896]{2,1,0:T(8,128)(2,1)}), bf16[16,32,896]{2,1,0:T(8,128)(2,1)S(1)}, u32[]{:S(2)}, u32[]{:S(2)}) async-start(bf16[16,32,896]{2,1,0:T(8,128)(2,1)} %bitcast.10), calls=%async_computation.4 | async-start | bytes 1835008 | tf_op jit(solution)/shard_map/all_to_all | solution.py:84
  210.6 17.8 %copy-start.1 = (bf16[512,896]{1,0:T(8,128)(2,1)S(1)}, bf16[512,896]{1,0:T(8,128)(2,1)}, u32[]{:S(2)}) copy-start(bf16[512,896]{1,0:T(8,128)(2,1)} %fusion.10) | copy-start | bytes 2752516
  224.5 17.0 %all-to-all-start.1 = ((bf16[16,32,896]{2,1,0:T(8,128)(2,1)}), bf16[16,32,896]{2,1,0:T(8,128)(2,1)S(1)}, u32[]{:S(2)}, u32[]{:S(2)}) async-start(bf16[16,32,896]{2,1,0:T(8,128)(2,1)} %bitcast.5), calls=%async_computation.1 | async-start | bytes 1835008 | tf_op jit(solution)/shard_map/all_to_all | solution.py:74
  237.6 5.8 %copy-start.2 = (f32[128,2]{1,0:T(8,128)S(1)}, f32[128,2]{1,0:T(8,128)}, u32[]{:S(2)}) copy-start(f32[128,2]{1,0:T(8,128)} %copy.53) | copy-start | bytes 3076
Sparse Core Ops, SparseCore 0:
  68.0 120.5 all-reduce.4
where the time goes:
time: 258 us; the launch traced here: 253 us
  waiting for transfers between devices  150 us (58%)
  matrix products  42.9 us (17%)
  starting transfers between devices  26 us (10%)
  between operations  14.2 us (6%)
  other arithmetic  12.2 us (5%)
  local copies, waits for them, and re-layouts  7.43 us (3%)
    psum x1, waiting for transfers between devices, per_device(): lax.psum(jnp.dot(expert_rows, up_local, preferred_element_type=jnp.float3...  118 us
    dot_general x2, matrix products, contract_last(): lax.dot_general(left, right, (((1,), (1,)), ((), ())), preferred_element_...  12.9 us
    dot_general x2, matrix products, contract_first(): lax.dot_general(left, right, (((0,), (0,)), ((), ())), preferred_element_...  12 us
    all_to_all x1, waiting for transfers between devices, per_device(): lax.all_to_all(sent_grads.reshape(experts, capacity, features), 'expert',...  11.1 us
    all_to_all x1, starting transfers between devices, per_device(): lax.all_to_all(slot_weight, 'expert', split_axis=0, concat_axis=0, tiled=...  7.58 us
    dot_general x1, matrix products, per_device(): jnp.dot(hidden, down_local, preferred_element_type=jnp.float32)  7.58 us
    dot_general x1, matrix products, per_device(): jnp.dot(expert_rows, up_local, preferred_element_type=jnp.float32)  6.74 us
    all_to_all x1, starting transfers between devices, per_device(): lax.all_to_all(row_grad.reshape(experts, capacity, features), 'expert', s...  6.53 us
  transfers between devices with their start and end apart: 6, of which 6 were waited for; matrix products, arithmetic and copies ran while one was open for 12% of the time, Pallas kernels for 0%

commit v1 on v0

v1 whole, which is shorter than its diff:
```python
import functools

import jax
import jax.numpy as jnp
from jax import lax
from jax.experimental import pallas as pl
from jax.experimental.pallas import tpu as pltpu
from jax.sharding import PartitionSpec as P

MESH = pl.DeviceIdType.MESH
F32 = jnp.float32
BF16 = jnp.bfloat16
NX = 4
NZ = 4
CAP = 32
SOURCES = tuple((s % NX, (s + s // NX) % NX) for s in range(NX * NX))
CHUNKS = ((0, 4), (4, 12), (12, 16))
ORDER = (
    "P01", "P10", "P00", "P11", "P21", "A01", "B01", "P20", "A10", "A00", "C01", "B10",
    "B00", "A11", "C10", "C00", "B11", "D10", "A21", "C11", "A20", "E10", "B20", "D11",
    "F10", "D00", "G10", "C20", "E11", "B21", "D20", "E00", "F11", "D01", "C21", "G11",
    "E20", "F00", "E01", "D21", "F20", "G00", "F01", "E21", "G20", "F21", "G01", "G21",
)
VMEM_LIMIT = 60 * 1024 * 1024


def contract_last(left, right):
    return lax.dot_general(left, right, (((1,), (1,)), ((), ())), preferred_element_type=F32)


def contract_first(left, right):
    return lax.dot_general(left, right, (((0,), (0,)), ((), ())), preferred_element_type=F32)


def column_tiles(width, tile=512):
    return [(start, min(start + tile, width)) for start in range(0, width, tile)]


def wrap(value, size):
    return lax.rem(value + size, size)


def moe_kernel(
    tokens_hbm, cotangent_hbm, routes, route_weights, plan, up_hbm, down_hbm,
    returned, rows_hbm, acts_hbm, placer, weighted,
    up, down, tokens, cotangent, sent, rows, part, core_out, core_in,
    first_out, first_in, second_out, second_in, acts, results,
    load_sem, own_sem, sent_sem, rows_sem, core_send, core_recv,
    first_send, first_recv, second_send, second_recv,
    near_send, near_recv, far_send, far_recv, mate_send, mate_recv,
    ret_send, ret_recv, store_sem,
):
    expert = lax.axis_index("expert")
    place = lax.axis_index("tensor")
    x, y = lax.div(expert, NX), lax.rem(expert, NX)
    z, core = lax.div(place, 2), lax.rem(place, 2)
    z_next, z_prev, z_far = wrap(z + 1, NZ), wrap(z - 1, NZ), wrap(z + 2, NZ)
    other = 1 - core
    n_tok, features = tokens.shape
    hidden_units = up.shape[1]
    split = ((hidden_units // 128 + 1) // 2) * 128
    tiles = column_tiles(hidden_units)
    half_a, half_b = pl.ds(0, split), pl.ds(split, hidden_units - split)
    n_experts, slots = NX * NX, NX * NX * CAP

    def at_z(which):
        return {"expert": expert, "tensor": which * 2 + core}

    next_chip, prev_chip = at_z(z_next), at_z(z_prev)
    mate = {"expert": expert, "tensor": z * 2 + other}
    owners = [wrap(x - dx, NX) * NX + wrap(y - dy, NX) for dx, dy in SOURCES]
    sources = [wrap(x + dx, NX) * NX + wrap(y + dy, NX) for dx, dy in SOURCES]

    def remote(src, dst, send, recv, device):
        return pltpu.make_async_remote_copy(
            src_ref=src, dst_ref=dst, send_sem=send, recv_sem=recv, device_id=device, device_id_type=MESH
        )

    def await_received(ref, sem):
        remote(ref, ref, sem, sem, mate).wait_recv()

    def await_sent(ref, sem):
        remote(ref, ref, sem, sem, mate).wait_send()

    barrier = pltpu.get_barrier_semaphore()
    load_tokens = pltpu.make_async_copy(tokens_hbm, tokens, load_sem.at[2])
    load_cotangent = pltpu.make_async_copy(cotangent_hbm, cotangent, load_sem.at[3])
    load_up = pltpu.make_async_copy(up_hbm.at[0], up, load_sem.at[0])
    load_down = pltpu.make_async_copy(down_hbm.at[0], down, load_sem.at[1])
    for load in (load_tokens, load_cotangent, load_up, load_down):
        load.start()
    for peer in sources[1:]:
        pl.semaphore_signal(barrier, inc=1, device_id={"expert": peer, "tensor": place}, device_id_type=MESH)
    for device in (next_chip, prev_chip, mate):
        pl.semaphore_signal(barrier, inc=1, device_id=device, device_id_type=MESH)

    expert_id = lax.broadcasted_iota(jnp.int32, (n_experts, n_tok), 0)
    first, second = routes[0:1, :], routes[1:2, :]
    named_first = (expert_id == first).astype(F32)
    named_second = (expert_id == second).astype(F32)
    before = lax.broadcasted_iota(jnp.int32, (n_tok, n_tok), 0) < lax.broadcasted_iota(jnp.int32, (n_tok, n_tok), 1)
    earlier = jnp.dot(
        (named_first + named_second).astype(BF16), before.astype(F32).astype(BF16), preferred_element_type=F32
    )
    limit = jnp.zeros((n_experts, 1), F32)
    expert_one = lax.broadcasted_iota(jnp.int32, (n_experts, 1), 0)
    for which in range(n_experts):
        limit = limit + jnp.where(expert_one == which, plan[which].astype(F32), 0.0)
    slot_id = lax.broadcasted_iota(jnp.int32, (slots, n_tok), 0).astype(F32)
    ones = jnp.zeros((slots, n_tok), F32)
    scaled = jnp.zeros((slots, n_tok), F32)
    pairs = ((first, named_first, earlier), (second, named_second, earlier + named_first))
    for k, (named_id, named, count) in enumerate(pairs):
        position = jnp.sum(count * named, axis=0, keepdims=True)
        allowed = jnp.sum(limit * named, axis=0, keepdims=True)
        slot = jnp.where(position < allowed, named_id.astype(F32) * CAP + position, -1.0)
        hit = slot_id == slot
        ones = ones + jnp.where(hit, 1.0, 0.0)
        scaled = scaled + jnp.where(hit, route_weights[k : k + 1, :].astype(F32), 0.0)
    placer[...] = ones.astype(BF16)
    weighted[...] = scaled.astype(BF16)

    def source_rows(s, count=1):
        return pl.ds(s * CAP, count * CAP)

    def chunk_rows(c):
        lo, hi = CHUNKS[c]
        return pl.ds(lo * CAP, (hi - lo) * CAP)

    def block_size(c):
        lo, hi = CHUNKS[c]
        return (hi - lo) * CAP // (2 * NZ)

    def block(c, side, which, count=1):
        size = block_size(c)
        return pl.ds(pl.multiple_of(CHUNKS[c][0] * CAP + (side * NZ + which) * size, 16), count * size)

    def half_block(c, which, count=1):
        size = block_size(c)
        return pl.ds(pl.multiple_of(CHUNKS[c][0] * CAP // 2 + which * size, 16), count * size)

    def small_block(c):
        return pl.ds(CHUNKS[c][0] * CAP // (2 * NZ), block_size(c))

    def remote_sources(c):
        lo, hi = CHUNKS[c]
        return range(max(lo, 1), hi)

    def make_rows(c, k):
        matrix, picker = ((tokens, placer), (cotangent, weighted))[k]
        for s in range(*CHUNKS[c]):
            pick = pl.ds(pl.multiple_of(owners[s] * CAP, CAP), CAP)
            sent[k, source_rows(s), :] = jnp.dot(
                picker[pick, :], matrix[...], preferred_element_type=F32
            ).astype(BF16)
            if s == 0:
                own_rows(k).start()
            else:
                remote(
                    sent.at[k, source_rows(s)], rows.at[k, source_rows(s)], sent_sem.at[k], rows_sem.at[c, k],
                    {"expert": owners[s], "tensor": place},
                ).start()

    def own_rows(k):
        return pltpu.make_async_copy(sent.at[k, source_rows(0)], rows.at[k, source_rows(0)], own_sem.at[0, k])

    def own_back(k):
        return pltpu.make_async_copy(results.at[k, source_rows(0)], returned.at[k, expert], own_sem.at[1, k])

    def save_acts(c, k):
        return pltpu.make_async_copy(acts.at[k, chunk_rows(c)], acts_hbm.at[k, chunk_rows(c)], store_sem.at[0, c, k])

    def save_rows(k):
        return pltpu.make_async_copy(rows.at[k], rows_hbm.at[k], store_sem.at[1, 0, k])

    partial_order = [(int(step[1]), int(step[2])) for step in ORDER if step[0] == "A"]

    def stage_partial(c, k):
        if c == 0:
            own_rows(k).wait()
        if (c, k) == next((step_c, step_k) for step_c, step_k in partial_order if step_k == k):
            (load_up if k == 0 else load_down).wait()
        arriving = remote_sources(c)
        await_received(rows.at[k, source_rows(arriving[0], len(arriving))], rows_sem.at[c, k])
        taken = rows[k, chunk_rows(c), :]
        for lo, hi in tiles:
            if k == 0:
                product = jnp.dot(taken, up[:, lo:hi], preferred_element_type=F32)
            else:
                product = contract_last(taken, down[lo:hi, :])
            part[k, chunk_rows(c), lo:hi] = product
        away = half_block(c, 0, NZ)
        core_out[k, away, :] = part[k, block(c, other, 0, NZ), :].astype(BF16)
        remote(core_out.at[k, away], core_in.at[k, away], core_send.at[0], core_recv.at[c, k], mate).start()
        if c == len(CHUNKS) - 1:
            save_rows(k).start()

    def chip_sum(c, k, which, half):
        return part[k, block(c, core, which), half] + core_in[k, half_block(c, which), half].astype(F32)

    def send_second(c, k, side, half):
        remote(
            second_out.at[k, side, small_block(c), half], second_in.at[k, side, small_block(c), half],
            second_send.at[0], second_recv.at[c, k], next_chip if side == 0 else prev_chip,
        ).start()

    def stage_core(c, k):
        await_received(core_in.at[k, half_block(c, 0, NZ)], core_recv.at[c, k])
        here = small_block(c)
        for half, device in ((half_a, next_chip), (half_b, prev_chip)):
            first_out[k, here, half] = chip_sum(c, k, z_far, half).astype(BF16)
            remote(
                first_out.at[k, here, half], first_in.at[k, here, half], first_send.at[0], first_recv.at[c, k], device
            ).start()
        second_out[k, 0, here, half_b] = chip_sum(c, k, z_next, half_b).astype(BF16)
        send_second(c, k, 0, half_b)
        second_out[k, 1, here, half_a] = chip_sum(c, k, z_prev, half_a).astype(BF16)
        send_second(c, k, 1, half_a)

    def stage_relay(c, k):
        here = small_block(c)
        await_received(first_in.at[k, here], first_recv.at[c, k])
        for side, which, half in ((0, z_next, half_a), (1, z_prev, half_b)):
            total = chip_sum(c, k, which, half) + first_in[k, here, half].astype(F32)
            second_out[k, side, here, half] = total.astype(BF16)
            send_second(c, k, side, half)

    def stage_activate(c, k):
        here = small_block(c)
        await_received(second_in.at[k, :, here], second_recv.at[c, k])
        total = chip_sum(c, k, z, pl.ds(0, hidden_units))
        total = total + (second_in[k, 0, here, :].astype(F32) + second_in[k, 1, here, :].astype(F32))
        mine = block(c, core, z)
        if k == 0:
            part[0, mine, :] = total
            acts[0, mine, :] = (total * jax.nn.sigmoid(total)).astype(BF16)
        else:
            pre = part[0, mine, :]
            gate = jax.nn.sigmoid(pre)
            acts[1, mine, :] = (total * gate * (1.0 + pre * (1.0 - gate))).astype(BF16)
        ref = acts.at[k, mine]
        remote(ref, ref, near_send.at[0], near_recv.at[c, k], next_chip).start()
        remote(ref, ref, near_send.at[0], near_recv.at[c, k], prev_chip).start()
        remote(ref, ref, mate_send.at[0], mate_recv.at[c, k], mate).start()

    def stage_forward(c, k):
        await_received(acts.at[k, block(c, core, 0, 2)], near_recv.at[c, k])
        for which, half, device in ((z_prev, half_a, next_chip), (z_next, half_b, prev_chip)):
            ref = acts.at[k, block(c, core, which), half]
            remote(ref, ref, far_send.at[0], far_recv.at[c, k], device).start()
        for which in (z_prev, z_next):
            ref = acts.at[k, block(c, core, which)]
            remote(ref, ref, mate_send.at[0], mate_recv.at[c, k], mate).start()

    def stage_last(c, k):
        ref = acts.at[k, block(c, core, z_far)]
        await_received(ref, far_recv.at[c, k])
        remote(ref, ref, mate_send.at[0], mate_recv.at[c, k], mate).start()

    def stage_result(c, k):
        await_received(acts.at[k, block(c, other, 0, NZ)], mate_recv.at[c, k])
        taken = acts[k, chunk_rows(c), :]
        for lo, hi in column_tiles(features):
            if k == 0:
                product = jnp.dot(taken, down[:, lo:hi], preferred_element_type=F32)
            else:
                product = contract_last(taken, up[lo:hi, :])
            results[k, chunk_rows(c), lo:hi] = product.astype(BF16)
        if c == 0:
            own_back(k).start()
        for s in remote_sources(c):
            remote(
                results.at[k, source_rows(s)], returned.at[k, expert], ret_send.at[k], ret_recv.at[k],
                {"expert": sources[s], "tensor": place},
            ).start()
        save_acts(c, k).start()

    stages = {
        "P": make_rows, "A": stage_partial, "B": stage_core, "C": stage_relay, "D": stage_activate,
        "E": stage_forward, "F": stage_last, "G": stage_result,
    }

    load_tokens.wait()
    load_cotangent.wait()
    pl.semaphore_wait(barrier, n_experts - 1 + 3)
    for step in ORDER:
        stages[step[0]](int(step[1]), int(step[2]))

    for k in range(2):
        await_sent(sent.at[k, source_rows(1, n_experts - 1)], sent_sem.at[k])
        save_rows(k).wait()
        own_back(k).wait()
        for c in range(len(CHUNKS)):
            save_acts(c, k).wait()
    quarter = slots // NZ
    await_sent(core_out, core_send.at[0])
    await_sent(first_out, first_send.at[0])
    await_sent(second_out, second_send.at[0])
    await_sent(acts.at[:, pl.ds(0, quarter)], near_send.at[0])
    await_sent(acts.at[:, pl.ds(0, quarter // 2)], far_send.at[0])
    await_sent(acts.at[:, pl.ds(0, 2 * quarter)], mate_send.at[0])
    for k in range(2):
        await_received(returned.at[k, pl.ds(0, n_experts - 1)], ret_recv.at[k])
        await_sent(results.at[k, source_rows(1, n_experts - 1)], ret_send.at[k])


def weight_grad_kernel(
    rows_hbm, acts_hbm, returned_hbm, placer, weighted,
    layer_out, token_grad, up_grad, down_grad,
    rows, acts, returned, flipped, up_tile, down_tile, load_sem, acts_sem, store_sem,
):
    features = rows.shape[-1]
    hidden_units = acts.shape[-1]
    slots = rows.shape[1]
    tiles = column_tiles(hidden_units)
    loads = [pltpu.make_async_copy(rows_hbm.at[kind], rows.at[kind], load_sem.at[kind]) for kind in range(2)]
    loads[0].start()
    acts_loads = [
        [
            pltpu.make_async_copy(acts_hbm.at[kind, :, lo:hi], acts.at[kind, :, lo:hi], acts_sem.at[kind, index])
            for index, (lo, hi) in enumerate(tiles)
        ]
        for kind in range(2)
    ]
    for load in acts_loads[1]:
        load.start()
    loads[1].start()
    for load in acts_loads[0]:
        load.start()
    load_returned = pltpu.make_async_copy(returned_hbm, returned, load_sem.at[2])
    load_returned.start()
    stores = []
    loads[0].wait()
    flipped[...] = rows[0].T
    for index, (lo, hi) in enumerate(tiles):
        acts_loads[1][index].wait()
        up_tile[:, lo:hi] = jnp.dot(flipped[...], acts[1, :, lo:hi], preferred_element_type=F32).astype(BF16)
        store = pltpu.make_async_copy(up_tile.at[:, lo:hi], up_grad.at[0, :, lo:hi], store_sem.at[0, index])
        store.start()
        stores.append(store)
    loads[1].wait()
    for index, (lo, hi) in enumerate(tiles):
        acts_loads[0][index].wait()
        down_tile[lo:hi, :] = contract_first(acts[0, :, lo:hi], rows[1]).astype(BF16)
        store = pltpu.make_async_copy(down_tile.at[lo:hi, :], down_grad.at[0, lo:hi, :], store_sem.at[1, index])
        store.start()
        stores.append(store)
    load_returned.wait()
    layer_out[...] = contract_first(weighted[...], returned[0].reshape(slots, features)).astype(BF16)
    token_grad[...] = contract_first(placer[...], returned[1].reshape(slots, features)).astype(BF16)
    for store in stores:
        store.wait()


def per_device(tokens, cotangent, routes, route_weights, capacity_plan, up_weight, down_weight):
    n_tok, features = tokens.shape
    hidden_units = up_weight.shape[2]
    slots = NX * NX * CAP
    vmem = pl.BlockSpec(memory_space=pltpu.VMEM)
    hbm = pl.BlockSpec(memory_space=pl.ANY)
    dma = pltpu.SemaphoreType.DMA
    flops = 8 * slots * features * hidden_units
    n_chunks = len(CHUNKS)
    returned, rows, acts, placer, weighted = pl.pallas_call(
        moe_kernel,
        out_shape=(
            jax.ShapeDtypeStruct((2, NX * NX, CAP, features), BF16),
            jax.ShapeDtypeStruct((2, slots, features), BF16),
            jax.ShapeDtypeStruct((2, slots, hidden_units), BF16),
            jax.ShapeDtypeStruct((slots, n_tok), BF16),
            jax.ShapeDtypeStruct((slots, n_tok), BF16),
        ),
        in_specs=[hbm, hbm, vmem, vmem, pl.BlockSpec(memory_space=pltpu.SMEM), hbm, hbm],
        out_specs=(hbm, hbm, hbm, vmem, vmem),
        scratch_shapes=[
            pltpu.VMEM((features, hidden_units), BF16),
            pltpu.VMEM((hidden_units, features), BF16),
            pltpu.VMEM((n_tok, features), BF16),
            pltpu.VMEM((n_tok, features), BF16),
            pltpu.VMEM((2, slots, features), BF16),
            pltpu.VMEM((2, slots, features), BF16),
            pltpu.VMEM((2, slots, hidden_units), F32),
            pltpu.VMEM((2, slots // 2, hidden_units), BF16),
            pltpu.VMEM((2, slots // 2, hidden_units), BF16),
            pltpu.VMEM((2, slots // (2 * NZ), hidden_units), BF16),
            pltpu.VMEM((2, slots // (2 * NZ), hidden_units), BF16),
            pltpu.VMEM((2, 2, slots // (2 * NZ), hidden_units), BF16),
            pltpu.VMEM((2, 2, slots // (2 * NZ), hidden_units), BF16),
            pltpu.VMEM((2, slots, hidden_units), BF16),
            pltpu.VMEM((2, slots, features), BF16),
            dma((4,)),
            dma((2, 2)),
            dma((2,)),
            dma((n_chunks, 2)),
            dma((1,)),
            dma((n_chunks, 2)),
            dma((1,)),
            dma((n_chunks, 2)),
            dma((1,)),
            dma((n_chunks, 2)),
            dma((1,)),
            dma((n_chunks, 2)),
            dma((1,)),
            dma((n_chunks, 2)),
            dma((1,)),
            dma((n_chunks, 2)),
            dma((2,)),
            dma((2,)),
            dma((2, n_chunks, 2)),
        ],
        compiler_params=pltpu.CompilerParams(
            collective_id=0, has_side_effects=True, vmem_limit_bytes=VMEM_LIMIT
        ),
        cost_estimate=pl.CostEstimate(
            flops=flops, bytes_accessed=4 * features * hidden_units, transcendentals=slots * hidden_units // 8
        ),
        name="moe_exchange",
    )(tokens, cotangent, routes.T, route_weights.T, capacity_plan, up_weight, down_weight)
    n_tiles = len(column_tiles(hidden_units))
    layer_out, token_grad, up_grad, down_grad = pl.pallas_call(
        weight_grad_kernel,
        out_shape=(
            jax.ShapeDtypeStruct((n_tok, features), BF16),
            jax.ShapeDtypeStruct((n_tok, features), BF16),
            jax.ShapeDtypeStruct((1, features, hidden_units), BF16),
            jax.ShapeDtypeStruct((1, hidden_units, features), BF16),
        ),
        in_specs=[hbm, hbm, hbm, vmem, vmem],
        out_specs=(vmem, vmem, hbm, hbm),
        scratch_shapes=[
            pltpu.VMEM((2, slots, features), BF16),
            pltpu.VMEM((2, slots, hidden_units), BF16),
            pltpu.VMEM((2, NX * NX, CAP, features), BF16),
            pltpu.VMEM((features, slots), BF16),
            pltpu.VMEM((features, hidden_units), BF16),
            pltpu.VMEM((hidden_units, features), BF16),
            dma((3,)),
            dma((2, n_tiles)),
            dma((2, n_tiles)),
        ],
        compiler_params=pltpu.CompilerParams(vmem_limit_bytes=VMEM_LIMIT),
        cost_estimate=pl.CostEstimate(
            flops=flops // 2, bytes_accessed=4 * features * hidden_units, transcendentals=0
        ),
        name="weight_grads",
    )(rows, acts, returned, placer, weighted)
    return layer_out, token_grad, up_grad, down_grad


def solution(mesh):
    placed = (
        P("expert", "tensor"),
        P("expert", "tensor"),
        P("expert", None),
        P("expert", None),
        P(),
        P("expert", "tensor", None),
        P("expert", None, "tensor"),
    )
    return jax.shard_map(
        per_device,
        mesh=mesh,
        in_specs=placed,
        out_specs=(
            P("expert", "tensor"),
            P("expert", "tensor"),
            P("expert", "tensor", None),
            P("expert", None, "tensor"),
        ),
        check_vma=False,
    )
```

time: 258 us -> 97.8 us (0.38); the launches traced: 253 us -> 97.5 us
  waiting for transfers between devices: 150 us -> 0 us
  Pallas kernels: 0 us -> 96.7 us
  matrix products: 42.9 us -> 0 us
  starting transfers between devices: 26 us -> 0 us
  between operations: 14.2 us -> 0.8 us
  other arithmetic: 12.2 us -> 0 us
  local copies, waits for them, and re-layouts: 7.43 us -> 0 us
    psum x1 -> x0, waiting for transfers between devices: 118 us -> none  [per_device(): lax.psum(jnp.dot(expert_rows, up_local, preferred_element_type=jnp.float3...]
    pallas_call x0 -> x2, Pallas kernels: none -> 96.7 us  [the longest x1 84.6 us: per_device(): pl.pallas_call(moe_kernel, out_shape=(jax.ShapeDtypeStruct((2, NX * NX, C...]
    dot_general x8 -> x0, matrix products: 42.9 us -> none  [the longest x2 12.9 us: contract_last(): lax.dot_general(left, right, (((1,), (1,)), ((), ())), preferred_element_...]
    all_to_all x5 -> x0, waiting for transfers between devices: 32.4 us -> none  [the longest x1 11.1 us: per_device(): lax.all_to_all(sent_grads.reshape(experts, capacity, features), 'expert',...]
    all_to_all x5 -> x0, starting transfers between devices: 26 us -> none  [the longest x1 7.58 us: per_device(): lax.all_to_all(slot_weight, 'expert', split_axis=0, concat_axis=0, tiled=...]
    convert_element_type x8 -> x0, other arithmetic: 6.89 us -> none  [the longest x1 4.82 us: per_device(): (d_hidden * gate_sig * (1.0 + pre_act * (1.0 - gate_sig))).astype(jnp.bfl...]
    reduce_sum x3 -> x0, other arithmetic: 3.9 us -> none  [the longest x1 3 us: per_device(): jnp.sum(kept_float[:, :, None] * picked_grad, axis=1).astype(jnp.bfloat16)]
  transfers between devices with their start and end apart: 6 -> 0, of which waited for: 6 -> 0; matrix products, arithmetic and copies ran while one was open for 12% -> 0% of each run, Pallas kernels for 0% -> 0%
where the time goes in v1:
time: 97.8 us; the launch traced here: 97.5 us
  Pallas kernels  96.7 us (99%)
    pallas_call x1, Pallas kernels, per_device(): pl.pallas_call(moe_kernel, out_shape=(jax.ShapeDtypeStruct((2, NX * NX, C...  84.6 us
    pallas_call x1, Pallas kernels, per_device(): pl.pallas_call(weight_grad_kernel, out_shape=(jax.ShapeDtypeStruct((n_tok...  12.1 us

profile of v1, /device:TPU:1, one launch (start us, length us, event | category | flops | bytes accessed | tf_op | source)
XLA Modules:
  0.0 97.5 jit_solution(13585905201726298704)
XLA Ops:
  0.6 84.6 %moe_exchange.1 = (bf16[2,16,32,896]{3,2,1,0:T(8,128)(2,1)}, bf16[2,512,896]{2,1,0:T(8,128)(2,1)}, bf16[2,512,2432]{2,1,0:T(8,128)(2,1)}, bf16[512,128]{1,0:T(8,128)(2,1)}, bf16[512,128]{1,0:T(8,128)(2,1)}) custom-call(bf16[128,896]{1,0:T(8,128)(2,1)} %tokens_hbm.1, bf16[128,896]{1,0:T(8,128)(2,1)} %cotangent_hbm.1, s32[2,128]{1,0:T(2,128)} %bitcast.2, ...), custom_call_target="tpu_custom_call" | custom-call | flops 8925478912 | bytes 8716288 | tf_op jit(solution)/shard_map/moe_exchange/pallas_call | solution.py:364
  85.3 12.1 %weight_grads.1 = (bf16[128,896]{1,0:T(8,128)(2,1)}, bf16[128,896]{1,0:T(8,128)(2,1)}, bf16[1,896,2432]{2,1,0:T(8,128)(2,1)}, bf16[1,2432,896]{2,1,0:T(8,128)(2,1)}) custom-call(bf16[2,512,896]{2,1,0:T(8,128)(2,1)} %get-tuple-element.9.rows_hbm, bf16[2,512,2432]{2,1,0:T(8,128)(2,1)} %get-tuple-element.10.acts_hbm, ...), custom_call_target="tpu_custom_call" | custom-call | flops 4462739456 | bytes 8716288 | tf_op jit(solution)/shard_map/weight_grads/pallas_call | solution.py:420

commit v2 on v1

--- a/solution.py
+++ b/solution.py
@@ -16,12 +16,16 @@
 SOURCES = tuple((s % NX, (s + s // NX) % NX) for s in range(NX * NX))
 CHUNKS = ((0, 4), (4, 12), (12, 16))
 ORDER = (
-    "P01", "P10", "P00", "P11", "P21", "A01", "B01", "P20", "A10", "A00", "C01", "B10",
-    "B00", "A11", "C10", "C00", "B11", "D10", "A21", "C11", "A20", "E10", "B20", "D11",
-    "F10", "D00", "G10", "C20", "E11", "B21", "D20", "E00", "F11", "D01", "C21", "G11",
-    "E20", "F00", "E01", "D21", "F20", "G00", "F01", "E21", "G20", "F21", "G01", "G21",
+    "P01", "P00", "P10", "P11", "A01", "A00", "B01", "B00", "A10", "C00", "P20", "C01",
+    "D00", "D01", "E00", "B10", "P21", "C10", "E01", "A11", "D10", "A21", "F01", "E10",
+    "B11", "F00", "A20", "F10", "C11", "B21", "G00", "D11", "G01", "G10", "E11", "B20",
+    "F11", "C20", "C21", "D20", "D21", "G11", "E21", "X00", "F21", "E20", "F20", "G21",
+    "G20",
 )
+TILE = 512
+PIECES = 4
 VMEM_LIMIT = 60 * 1024 * 1024
+COMBINE_VMEM_LIMIT = 60 * 1024 * 1024
 
 
 def contract_last(left, right):
@@ -32,7 +36,7 @@
     return lax.dot_general(left, right, (((0,), (0,)), ((), ())), preferred_element_type=F32)
 
 
-def column_tiles(width, tile=512):
+def column_tiles(width, tile=TILE):
     return [(start, min(start + tile, width)) for start in range(0, width, tile)]
 
 
@@ -41,9 +45,9 @@
 
 
 def moe_kernel(
-    tokens_hbm, cotangent_hbm, routes, route_weights, plan, up_hbm, down_hbm,
-    returned, rows_hbm, acts_hbm, placer, weighted,
-    up, down, tokens, cotangent, sent, rows, part, core_out, core_in,
+    tokens_hbm, cotangent_hbm, routes_hbm, weights_hbm, plan_hbm, up_hbm, down_hbm,
+    returned, up_grad, down_grad, placer, weighted,
+    up, down, flipped, tokens, cotangent, routes, route_weights, plan, sent, rows, part, core_out, core_in,
     first_out, first_in, second_out, second_in, acts, results,
     load_sem, own_sem, sent_sem, rows_sem, core_send, core_recv,
     first_send, first_recv, second_send, second_recv,
@@ -87,12 +91,21 @@
     load_cotangent = pltpu.make_async_copy(cotangent_hbm, cotangent, load_sem.at[3])
     load_up = pltpu.make_async_copy(up_hbm.at[0], up, load_sem.at[0])
     load_down = pltpu.make_async_copy(down_hbm.at[0], down, load_sem.at[1])
-    for load in (load_tokens, load_cotangent, load_up, load_down):
+    load_routing = [
+        pltpu.make_async_copy(source, target, load_sem.at[4 + which])
+        for which, (source, target) in enumerate(
+            ((routes_hbm, routes), (weights_hbm, route_weights), (plan_hbm, plan))
+        )
+    ]
+    for load in (*load_routing, load_tokens, load_cotangent, load_up, load_down):
         load.start()
     for peer in sources[1:]:
         pl.semaphore_signal(barrier, inc=1, device_id={"expert": peer, "tensor": place}, device_id_type=MESH)
     for device in (next_chip, prev_chip, mate):
         pl.semaphore_signal(barrier, inc=1, device_id=device, device_id_type=MESH)
+
+    for load in load_routing:
+        load.wait()
 
     expert_id = lax.broadcasted_iota(jnp.int32, (n_experts, n_tok), 0)
     first, second = routes[0:1, :], routes[1:2, :]
@@ -102,10 +115,10 @@
     earlier = jnp.dot(
         (named_first + named_second).astype(BF16), before.astype(F32).astype(BF16), preferred_element_type=F32
     )
-    limit = jnp.zeros((n_experts, 1), F32)
-    expert_one = lax.broadcasted_iota(jnp.int32, (n_experts, 1), 0)
-    for which in range(n_experts):
-        limit = limit + jnp.where(expert_one == which, plan[which].astype(F32), 0.0)
+    diagonal = lax.broadcasted_iota(jnp.int32, (n_experts, n_experts), 0) == lax.broadcasted_iota(
+        jnp.int32, (n_experts, n_experts), 1
+    )
+    limit = jnp.sum(jnp.where(diagonal, plan[...].astype(F32), 0.0), axis=1, keepdims=True)
     slot_id = lax.broadcasted_iota(jnp.int32, (slots, n_tok), 0).astype(F32)
     ones = jnp.zeros((slots, n_tok), F32)
     scaled = jnp.zeros((slots, n_tok), F32)
@@ -166,12 +179,6 @@
 
     def own_back(k):
         return pltpu.make_async_copy(results.at[k, source_rows(0)], returned.at[k, expert], own_sem.at[1, k])
-
-    def save_acts(c, k):
-        return pltpu.make_async_copy(acts.at[k, chunk_rows(c)], acts_hbm.at[k, chunk_rows(c)], store_sem.at[0, c, k])
-
-    def save_rows(k):
-        return pltpu.make_async_copy(rows.at[k], rows_hbm.at[k], store_sem.at[1, 0, k])
 
     partial_order = [(int(step[1]), int(step[2])) for step in ORDER if step[0] == "A"]
 
@@ -192,8 +199,6 @@
         away = half_block(c, 0, NZ)
         core_out[k, away, :] = part[k, block(c, other, 0, NZ), :].astype(BF16)
         remote(core_out.at[k, away], core_in.at[k, away], core_send.at[0], core_recv.at[c, k], mate).start()
-        if c == len(CHUNKS) - 1:
-            save_rows(k).start()
 
     def chip_sum(c, k, which, half):
         return part[k, block(c, core, which), half] + core_in[k, half_block(c, which), half].astype(F32)
@@ -273,11 +278,33 @@
                 results.at[k, source_rows(s)], returned.at[k, expert], ret_send.at[k], ret_recv.at[k],
                 {"expert": sources[s], "tensor": place},
             ).start()
-        save_acts(c, k).start()
+
+    def stage_flip(c, k):
+        flipped[...] = rows[0].T
+
+    def make_up_grad(pick):
+        up[:, pick] = jnp.dot(flipped[...], acts[1, :, pick], preferred_element_type=F32).astype(BF16)
+        pltpu.make_async_copy(up.at[:, pick], up_grad.at[0, :, pick], store_sem.at[0]).start()
+
+    def make_down_grad(pick):
+        down[pick, :] = contract_first(acts[0, :, pick], rows[1]).astype(BF16)
+        pltpu.make_async_copy(down.at[pick], down_grad.at[0, pick], store_sem.at[1]).start()
+
+    def make_weight_grads():
+        whole = hidden_units // TILE
+        rest = pl.ds(whole * TILE, hidden_units - whole * TILE)
+        for make in (make_up_grad, make_down_grad):
+
+            def body(t, carry, make=make):
+                make(pl.ds(pl.multiple_of(t * TILE, TILE), TILE))
+                return carry
+
+            lax.fori_loop(0, whole, body, 0)
+            make(rest)
 
     stages = {
         "P": make_rows, "A": stage_partial, "B": stage_core, "C": stage_relay, "D": stage_activate,
-        "E": stage_forward, "F": stage_last, "G": stage_result,
+        "E": stage_forward, "F": stage_last, "G": stage_result, "X": stage_flip,
     }
 
     load_tokens.wait()
@@ -285,13 +312,11 @@
     pl.semaphore_wait(barrier, n_experts - 1 + 3)
     for step in ORDER:
         stages[step[0]](int(step[1]), int(step[2]))
+    make_weight_grads()
 
     for k in range(2):
         await_sent(sent.at[k, source_rows(1, n_experts - 1)], sent_sem.at[k])
-        save_rows(k).wait()
         own_back(k).wait()
-        for c in range(len(CHUNKS)):
-            save_acts(c, k).wait()
     quarter = slots // NZ
     await_sent(core_out, core_send.at[0])
     await_sent(first_out, first_send.at[0])
@@ -302,54 +327,60 @@
     for k in range(2):
         await_received(returned.at[k, pl.ds(0, n_experts - 1)], ret_recv.at[k])
         await_sent(results.at[k, source_rows(1, n_experts - 1)], ret_send.at[k])
-
-
-def weight_grad_kernel(
-    rows_hbm, acts_hbm, returned_hbm, placer, weighted,
-    layer_out, token_grad, up_grad, down_grad,
-    rows, acts, returned, flipped, up_tile, down_tile, load_sem, acts_sem, store_sem,
+    pltpu.make_async_copy(up, up_grad.at[0], store_sem.at[0]).wait()
+    pltpu.make_async_copy(down, down_grad.at[0], store_sem.at[1]).wait()
+
+
+def combine_kernel(
+    returned_hbm, placer_hbm, weighted_hbm, up_hbm, down_hbm,
+    layer_hbm, token_hbm, up_grad, down_grad,
+    returned, placer, weighted, layer_out, token_grad, up, down, load_sem, out_sem, in_sem, copy_sem,
 ):
-    features = rows.shape[-1]
-    hidden_units = acts.shape[-1]
-    slots = rows.shape[1]
-    tiles = column_tiles(hidden_units)
-    loads = [pltpu.make_async_copy(rows_hbm.at[kind], rows.at[kind], load_sem.at[kind]) for kind in range(2)]
-    loads[0].start()
-    acts_loads = [
-        [
-            pltpu.make_async_copy(acts_hbm.at[kind, :, lo:hi], acts.at[kind, :, lo:hi], acts_sem.at[kind, index])
-            for index, (lo, hi) in enumerate(tiles)
-        ]
-        for kind in range(2)
+    slots, features = placer.shape[0], layer_out.shape[1]
+    first = [
+        pltpu.make_async_copy(weighted_hbm, weighted, load_sem.at[0]),
+        pltpu.make_async_copy(returned_hbm.at[0], returned.at[0], load_sem.at[1]),
     ]
-    for load in acts_loads[1]:
+    second = [
+        pltpu.make_async_copy(placer_hbm, placer, load_sem.at[2]),
+        pltpu.make_async_copy(returned_hbm.at[1], returned.at[1], load_sem.at[3]),
+    ]
+    pieces = []
+    for which, (source, between, target) in enumerate(((up_hbm, up, up_grad), (down_hbm, down, down_grad))):
+        size = between.shape[0] // PIECES
+        for piece in range(PIECES):
+            pick = pl.ds(piece * size, size)
+            pieces.append(
+                (
+                    pltpu.make_async_copy(source.at[0, pick], between.at[pick], in_sem.at[which, piece]),
+                    pltpu.make_async_copy(between.at[pick], target.at[0, pick], copy_sem.at[which, piece]),
+                )
+            )
+    outs = [
+        pltpu.make_async_copy(layer_out, layer_hbm, out_sem.at[0]),
+        pltpu.make_async_copy(token_grad, token_hbm, out_sem.at[1]),
+    ]
+    for load in (pieces[0][0], *first, pieces[1][0], *second, *(piece[0] for piece in pieces[2:])):
         load.start()
-    loads[1].start()
-    for load in acts_loads[0]:
-        load.start()
-    load_returned = pltpu.make_async_copy(returned_hbm, returned, load_sem.at[2])
-    load_returned.start()
-    stores = []
-    loads[0].wait()
-    flipped[...] = rows[0].T
-    for index, (lo, hi) in enumerate(tiles):
-        acts_loads[1][index].wait()
-        up_tile[:, lo:hi] = jnp.dot(flipped[...], acts[1, :, lo:hi], preferred_element_type=F32).astype(BF16)
-        store = pltpu.make_async_copy(up_tile.at[:, lo:hi], up_grad.at[0, :, lo:hi], store_sem.at[0, index])
-        store.start()
-        stores.append(store)
-    loads[1].wait()
-    for index, (lo, hi) in enumerate(tiles):
-        acts_loads[0][index].wait()
-        down_tile[lo:hi, :] = contract_first(acts[0, :, lo:hi], rows[1]).astype(BF16)
-        store = pltpu.make_async_copy(down_tile.at[lo:hi, :], down_grad.at[0, lo:hi, :], store_sem.at[1, index])
-        store.start()
-        stores.append(store)
-    load_returned.wait()
+
+    def pass_on(some):
+        for load, store in some:
+            load.wait()
+            store.start()
+
+    pass_on(pieces[:1])
+    for load in first:
+        load.wait()
     layer_out[...] = contract_first(weighted[...], returned[0].reshape(slots, features)).astype(BF16)
+    outs[0].start()
+    pass_on(pieces[1:2])
+    for load in second:
+        load.wait()
     token_grad[...] = contract_first(placer[...], returned[1].reshape(slots, features)).astype(BF16)
-    for store in stores:
-        store.wait()
+    outs[1].start()
+    pass_on(pieces[2:])
+    for copy in (*outs, *(piece[1] for piece in pieces)):
+        copy.wait()
 
 
 def per_device(tokens, cotangent, routes, route_weights, capacity_plan, up_weight, down_weight):
@@ -359,24 +390,28 @@
     vmem = pl.BlockSpec(memory_space=pltpu.VMEM)
     hbm = pl.BlockSpec(memory_space=pl.ANY)
     dma = pltpu.SemaphoreType.DMA
-    flops = 8 * slots * features * hidden_units
+    flops = 12 * slots * features * hidden_units
     n_chunks = len(CHUNKS)
-    returned, rows, acts, placer, weighted = pl.pallas_call(
+    returned, up_made, down_made, placer, weighted = pl.pallas_call(
         moe_kernel,
         out_shape=(
             jax.ShapeDtypeStruct((2, NX * NX, CAP, features), BF16),
-            jax.ShapeDtypeStruct((2, slots, features), BF16),
-            jax.ShapeDtypeStruct((2, slots, hidden_units), BF16),
+            jax.ShapeDtypeStruct((1, features, hidden_units), BF16),
+            jax.ShapeDtypeStruct((1, hidden_units, features), BF16),
             jax.ShapeDtypeStruct((slots, n_tok), BF16),
             jax.ShapeDtypeStruct((slots, n_tok), BF16),
         ),
-        in_specs=[hbm, hbm, vmem, vmem, pl.BlockSpec(memory_space=pltpu.SMEM), hbm, hbm],
+        in_specs=[pl.BlockSpec(memory_space=pltpu.HBM)] * 7,
         out_specs=(hbm, hbm, hbm, vmem, vmem),
         scratch_shapes=[
             pltpu.VMEM((features, hidden_units), BF16),
             pltpu.VMEM((hidden_units, features), BF16),
+            pltpu.VMEM((features, slots), BF16),
             pltpu.VMEM((n_tok, features), BF16),
             pltpu.VMEM((n_tok, features), BF16),
+            pltpu.VMEM((2, n_tok), jnp.int32),
+            pltpu.VMEM((2, n_tok), BF16),
+            pltpu.VMEM((1, NX * NX), jnp.int32),
             pltpu.VMEM((2, slots, features), BF16),
             pltpu.VMEM((2, slots, features), BF16),
             pltpu.VMEM((2, slots, hidden_units), F32),
@@ -388,7 +423,7 @@
             pltpu.VMEM((2, 2, slots // (2 * NZ), hidden_units), BF16),
             pltpu.VMEM((2, slots, hidden_units), BF16),
             pltpu.VMEM((2, slots, features), BF16),
-            dma((4,)),
+            dma((7,)),
             dma((2, 2)),
             dma((2,)),
             dma((n_chunks, 2)),
@@ -406,7 +441,7 @@
             dma((n_chunks, 2)),
             dma((2,)),
             dma((2,)),
-            dma((2, n_chunks, 2)),
+            dma((2,)),
         ],
         compiler_params=pltpu.CompilerParams(
             collective_id=0, has_side_effects=True, vmem_limit_bytes=VMEM_LIMIT
@@ -415,36 +450,36 @@
             flops=flops, bytes_accessed=4 * features * hidden_units, transcendentals=slots * hidden_units // 8
         ),
         name="moe_exchange",
-    )(tokens, cotangent, routes.T, route_weights.T, capacity_plan, up_weight, down_weight)
-    n_tiles = len(column_tiles(hidden_units))
-    layer_out, token_grad, up_grad, down_grad = pl.pallas_call(
-        weight_grad_kernel,
+    )(tokens, cotangent, routes.T, route_weights.T, capacity_plan[None], up_weight, down_weight)
+    return pl.pallas_call(
+        combine_kernel,
         out_shape=(
             jax.ShapeDtypeStruct((n_tok, features), BF16),
             jax.ShapeDtypeStruct((n_tok, features), BF16),
             jax.ShapeDtypeStruct((1, features, hidden_units), BF16),
             jax.ShapeDtypeStruct((1, hidden_units, features), BF16),
         ),
-        in_specs=[hbm, hbm, hbm, vmem, vmem],
-        out_specs=(vmem, vmem, hbm, hbm),
+        in_specs=[hbm] * 5,
+        out_specs=(hbm,) * 4,
         scratch_shapes=[
-            pltpu.VMEM((2, slots, features), BF16),
-            pltpu.VMEM((2, slots, hidden_units), BF16),
             pltpu.VMEM((2, NX * NX, CAP, features), BF16),
-            pltpu.VMEM((features, slots), BF16),
+            pltpu.VMEM((slots, n_tok), BF16),
+            pltpu.VMEM((slots, n_tok), BF16),
+            pltpu.VMEM((n_tok, features), BF16),
+            pltpu.VMEM((n_tok, features), BF16),
             pltpu.VMEM((features, hidden_units), BF16),
             pltpu.VMEM((hidden_units, features), BF16),
-            dma((3,)),
-            dma((2, n_tiles)),
-            dma((2, n_tiles)),
+            dma((4,)),
+            dma((2,)),
+            dma((2, PIECES)),
+            dma((2, PIECES)),
         ],
-        compiler_params=pltpu.CompilerParams(vmem_limit_bytes=VMEM_LIMIT),
+        compiler_params=pltpu.CompilerParams(vmem_limit_bytes=COMBINE_VMEM_LIMIT),
         cost_estimate=pl.CostEstimate(
-            flops=flops // 2, bytes_accessed=4 * features * hidden_units, transcendentals=0
+            flops=4 * slots * n_tok * features, bytes_accessed=8 * features * hidden_units, transcendentals=0
         ),
-        name="weight_grads",
-    )(rows, acts, returned, placer, weighted)
-    return layer_out, token_grad, up_grad, down_grad
+        name="combine",
+    )(returned, placer, weighted, up_made, down_made)
 
 
 def solution(mesh):

time: 97.8 us -> 107 us (1.094)
  Pallas kernels: 96.7 us -> 106 us
    pallas_call x1, Pallas kernels: 84.6 us -> 98.4 us  [per_device(): pl.pallas_call(moe_kernel, out_shape=(jax.ShapeDtypeStruct((2, NX * NX, C...]
    pallas_call x1, Pallas kernels: 12.1 us -> 7.48 us  [per_device(): pl.pallas_call(combine_kernel, out_shape=(jax.ShapeDtypeStruct((n_tok, fe...]
where the time goes in v2:
time: 107 us
  Pallas kernels  106 us (99%)
    pallas_call x1, Pallas kernels, per_device(): pl.pallas_call(moe_kernel, out_shape=(jax.ShapeDtypeStruct((2, NX * NX, C...  98.4 us
    pallas_call x1, Pallas kernels, per_device(): pl.pallas_call(combine_kernel, out_shape=(jax.ShapeDtypeStruct((n_tok, fe...  7.48 us

profile of v2, /device:TPU:1, one launch (start us, length us, event | category | flops | bytes accessed | tf_op | source)
XLA Modules:
  0.0 106.7 jit_solution(10610078330172261887)
XLA Ops:
  0.6 98.4 %moe_exchange.1 = (bf16[2,16,32,896]{3,2,1,0:T(8,128)(2,1)}, bf16[1,896,2432]{2,1,0:T(8,128)(2,1)}, bf16[1,2432,896]{2,1,0:T(8,128)(2,1)}, bf16[512,128]{1,0:T(8,128)(2,1)}, bf16[512,128]{1,0:T(8,128)(2,1)}) custom-call(bf16[128,896]{1,0:T(8,128)(2,1)} %tokens_hbm.1, bf16[128,896]{1,0:T(8,128)(2,1)} %cotangent_hbm.1, s32[2,128]{1,0:T(2,128)} %bitcast.3, ...), custom_call_target="tpu_custom_call" | custom-call | flops 13388218368 | bytes 8716288 | tf_op jit(solution)/shard_map/moe_exchange/pallas_call | solution.py:395
  99.0 7.5 %combine.1 = (bf16[128,896]{1,0:T(8,128)(2,1)}, bf16[128,896]{1,0:T(8,128)(2,1)}, bf16[1,896,2432]{2,1,0:T(8,128)(2,1)}, bf16[1,2432,896]{2,1,0:T(8,128)(2,1)}) custom-call(bf16[2,16,32,896]{3,2,1,0:T(8,128)(2,1)} %get-tuple-element.9.returned_hbm, bf16[512,128]{1,0:T(8,128)(2,1)} %get-tuple-element.10.placer_hbm, ...), custom_call_target="tpu_custom_call" | custom-call | flops 234881024 | bytes 17432576 | tf_op jit(solution)/shard_map/combine/pallas_call | solution.py:454

commit v3 on v2

--- a/solution.py
+++ b/solution.py
@@ -16,11 +16,11 @@
 SOURCES = tuple((s % NX, (s + s // NX) % NX) for s in range(NX * NX))
 CHUNKS = ((0, 4), (4, 12), (12, 16))
 ORDER = (
-    "P01", "P00", "P10", "P11", "A01", "A00", "B01", "B00", "A10", "C00", "P20", "C01",
-    "D00", "D01", "E00", "B10", "P21", "C10", "E01", "A11", "D10", "A21", "F01", "E10",
-    "B11", "F00", "A20", "F10", "C11", "B21", "G00", "D11", "G01", "G10", "E11", "B20",
-    "F11", "C20", "C21", "D20", "D21", "G11", "E21", "X00", "F21", "E20", "F20", "G21",
-    "G20",
+    "P01", "P00", "P10", "A01", "B01", "P11", "C01", "A00", "A10", "B10", "B00", "P20",
+    "C10", "A11", "B11", "D10", "C11", "A20", "P21", "B20", "E10", "D11", "C00", "A21",
+    "F10", "B21", "C20", "E11", "G10", "D00", "D20", "F11", "D01", "C21", "G11", "E20",
+    "E00", "E01", "D21", "F20", "G20", "F01", "E21", "X00", "F00", "G01", "G00", "F21",
+    "G21",
 )
 TILE = 512
 PIECES = 4
@@ -246,20 +246,16 @@
         ref = acts.at[k, mine]
         remote(ref, ref, near_send.at[0], near_recv.at[c, k], next_chip).start()
         remote(ref, ref, near_send.at[0], near_recv.at[c, k], prev_chip).start()
-        remote(ref, ref, mate_send.at[0], mate_recv.at[c, k], mate).start()
 
     def stage_forward(c, k):
         await_received(acts.at[k, block(c, core, 0, 2)], near_recv.at[c, k])
         for which, half, device in ((z_prev, half_a, next_chip), (z_next, half_b, prev_chip)):
             ref = acts.at[k, block(c, core, which), half]
             remote(ref, ref, far_send.at[0], far_recv.at[c, k], device).start()
-        for which in (z_prev, z_next):
-            ref = acts.at[k, block(c, core, which)]
-            remote(ref, ref, mate_send.at[0], mate_recv.at[c, k], mate).start()
 
     def stage_last(c, k):
-        ref = acts.at[k, block(c, core, z_far)]
-        await_received(ref, far_recv.at[c, k])
+        await_received(acts.at[k, block(c, core, z_far)], far_recv.at[c, k])
+        ref = acts.at[k, block(c, core, 0, NZ)]
         remote(ref, ref, mate_send.at[0], mate_recv.at[c, k], mate).start()
 
     def stage_result(c, k):

time: 107 us -> 93.2 us (0.87)
  Pallas kernels: 106 us -> 92.3 us
    pallas_call x1, Pallas kernels: 98.4 us -> 84.9 us  [per_device(): pl.pallas_call(moe_kernel, out_shape=(jax.ShapeDtypeStruct((2, NX * NX, C...]
where the time goes in v3:
time: 93.2 us; the launch traced here: 93.1 us
  Pallas kernels  92.3 us (99%)
    pallas_call x1, Pallas kernels, per_device(): pl.pallas_call(moe_kernel, out_shape=(jax.ShapeDtypeStruct((2, NX * NX, C...  84.9 us
    pallas_call x1, Pallas kernels, per_device(): pl.pallas_call(combine_kernel, out_shape=(jax.ShapeDtypeStruct((n_tok, fe...  7.48 us

profile of v3, /device:TPU:1, one launch (start us, length us, event | category | flops | bytes accessed | tf_op | source)
XLA Modules:
  0.0 93.1 jit_solution(14446652460299232954)
XLA Ops:
  0.6 84.9 %moe_exchange.1 = (bf16[2,16,32,896]{3,2,1,0:T(8,128)(2,1)}, bf16[1,896,2432]{2,1,0:T(8,128)(2,1)}, bf16[1,2432,896]{2,1,0:T(8,128)(2,1)}, bf16[512,128]{1,0:T(8,128)(2,1)}, bf16[512,128]{1,0:T(8,128)(2,1)}) custom-call(bf16[128,896]{1,0:T(8,128)(2,1)} %tokens_hbm.1, bf16[128,896]{1,0:T(8,128)(2,1)} %cotangent_hbm.1, s32[2,128]{1,0:T(2,128)} %bitcast.3, ...), custom_call_target="tpu_custom_call" | custom-call | flops 13388218368 | bytes 8716288 | tf_op jit(solution)/shard_map/moe_exchange/pallas_call | solution.py:391
  85.5 7.5 %combine.1 = (bf16[128,896]{1,0:T(8,128)(2,1)}, bf16[128,896]{1,0:T(8,128)(2,1)}, bf16[1,896,2432]{2,1,0:T(8,128)(2,1)}, bf16[1,2432,896]{2,1,0:T(8,128)(2,1)}) custom-call(bf16[2,16,32,896]{3,2,1,0:T(8,128)(2,1)} %get-tuple-element.9.returned_hbm, bf16[512,128]{1,0:T(8,128)(2,1)} %get-tuple-element.10.placer_hbm, ...), custom_call_target="tpu_custom_call" | custom-call | flops 234881024 | bytes 17432576 | tf_op jit(solution)/shard_map/combine/pallas_call | solution.py:450

commit v4 on v3

--- a/solution.py
+++ b/solution.py
@@ -16,11 +16,11 @@
 SOURCES = tuple((s % NX, (s + s // NX) % NX) for s in range(NX * NX))
 CHUNKS = ((0, 4), (4, 12), (12, 16))
 ORDER = (
-    "P01", "P00", "P10", "A01", "B01", "P11", "C01", "A00", "A10", "B10", "B00", "P20",
-    "C10", "A11", "B11", "D10", "C11", "A20", "P21", "B20", "E10", "D11", "C00", "A21",
-    "F10", "B21", "C20", "E11", "G10", "D00", "D20", "F11", "D01", "C21", "G11", "E20",
-    "E00", "E01", "D21", "F20", "G20", "F01", "E21", "X00", "F00", "G01", "G00", "F21",
-    "G21",
+    "P01", "P00", "P10", "A01", "A00", "P11", "B01", "A10", "B00", "B10", "C00", "C01",
+    "A11", "C10", "P21", "B11", "D10", "C11", "P20", "D00", "E10", "A20", "B20", "D11",
+    "F10", "D01", "A21", "G10", "C20", "E11", "B21", "D20", "F11", "E01", "C21", "E00",
+    "G11", "E20", "F01", "D21", "F20", "X00", "F00", "G01", "E21", "G20", "F21", "G00",
+    "Y00", "G21",
 )
 TILE = 512
 PIECES = 4
@@ -46,13 +46,13 @@
 
 def moe_kernel(
     tokens_hbm, cotangent_hbm, routes_hbm, weights_hbm, plan_hbm, up_hbm, down_hbm,
-    returned, up_grad, down_grad, placer, weighted,
-    up, down, flipped, tokens, cotangent, routes, route_weights, plan, sent, rows, part, core_out, core_in,
+    returned, slope_hbm, flipped_hbm, down_grad, placer_hbm, weighted_hbm,
+    up, down, flipped, placer, weighted, tokens, cotangent, routes, route_weights, plan, sent, rows, part, core_out, core_in,
     first_out, first_in, second_out, second_in, acts, results,
     load_sem, own_sem, sent_sem, rows_sem, core_send, core_recv,
     first_send, first_recv, second_send, second_recv,
     near_send, near_recv, far_send, far_recv, mate_send, mate_recv,
-    ret_send, ret_recv, store_sem,
+    ret_send, ret_recv, store_sem, slope_sem,
 ):
     expert = lax.axis_index("expert")
     place = lax.axis_index("tensor")
@@ -161,18 +161,17 @@
 
     def make_rows(c, k):
         matrix, picker = ((tokens, placer), (cotangent, weighted))[k]
-        for s in range(*CHUNKS[c]):
-            pick = pl.ds(pl.multiple_of(owners[s] * CAP, CAP), CAP)
-            sent[k, source_rows(s), :] = jnp.dot(
-                picker[pick, :], matrix[...], preferred_element_type=F32
-            ).astype(BF16)
-            if s == 0:
-                own_rows(k).start()
-            else:
-                remote(
-                    sent.at[k, source_rows(s)], rows.at[k, source_rows(s)], sent_sem.at[k], rows_sem.at[c, k],
-                    {"expert": owners[s], "tensor": place},
-                ).start()
+        picked = [picker[pl.ds(pl.multiple_of(owners[s] * CAP, CAP), CAP), :] for s in range(*CHUNKS[c])]
+        sent[k, chunk_rows(c), :] = jnp.dot(
+            jnp.concatenate(picked, axis=0), matrix[...], preferred_element_type=F32
+        ).astype(BF16)
+        if c == 0:
+            own_rows(k).start()
+        for s in remote_sources(c):
+            remote(
+                sent.at[k, source_rows(s)], rows.at[k, source_rows(s)], sent_sem.at[k], rows_sem.at[c, k],
+                {"expert": owners[s], "tensor": place},
+            ).start()
 
     def own_rows(k):
         return pltpu.make_async_copy(sent.at[k, source_rows(0)], rows.at[k, source_rows(0)], own_sem.at[0, k])
@@ -212,22 +211,25 @@
     def stage_core(c, k):
         await_received(core_in.at[k, half_block(c, 0, NZ)], core_recv.at[c, k])
         here = small_block(c)
+        for half in (half_a, half_b):
+            first_out[k, here, half] = chip_sum(c, k, z_far, half).astype(BF16)
+        second_out[k, 0, here, half_b] = chip_sum(c, k, z_next, half_b).astype(BF16)
+        second_out[k, 1, here, half_a] = chip_sum(c, k, z_prev, half_a).astype(BF16)
         for half, device in ((half_a, next_chip), (half_b, prev_chip)):
-            first_out[k, here, half] = chip_sum(c, k, z_far, half).astype(BF16)
             remote(
                 first_out.at[k, here, half], first_in.at[k, here, half], first_send.at[0], first_recv.at[c, k], device
             ).start()
-        second_out[k, 0, here, half_b] = chip_sum(c, k, z_next, half_b).astype(BF16)
         send_second(c, k, 0, half_b)
-        second_out[k, 1, here, half_a] = chip_sum(c, k, z_prev, half_a).astype(BF16)
         send_second(c, k, 1, half_a)
 
     def stage_relay(c, k):
         here = small_block(c)
+        relays = ((0, z_next, half_a), (1, z_prev, half_b))
         await_received(first_in.at[k, here], first_recv.at[c, k])
-        for side, which, half in ((0, z_next, half_a), (1, z_prev, half_b)):
+        for side, which, half in relays:
             total = chip_sum(c, k, which, half) + first_in[k, here, half].astype(F32)
             second_out[k, side, here, half] = total.astype(BF16)
+        for side, which, half in relays:
             send_second(c, k, side, half)
 
     def stage_activate(c, k):
@@ -274,45 +276,44 @@
                 results.at[k, source_rows(s)], returned.at[k, expert], ret_send.at[k], ret_recv.at[k],
                 {"expert": sources[s], "tensor": place},
             ).start()
+        if k == 1:
+            save_slope(c).start()
 
     def stage_flip(c, k):
         flipped[...] = rows[0].T
-
-    def make_up_grad(pick):
-        up[:, pick] = jnp.dot(flipped[...], acts[1, :, pick], preferred_element_type=F32).astype(BF16)
-        pltpu.make_async_copy(up.at[:, pick], up_grad.at[0, :, pick], store_sem.at[0]).start()
-
-    def make_down_grad(pick):
-        down[pick, :] = contract_first(acts[0, :, pick], rows[1]).astype(BF16)
-        pltpu.make_async_copy(down.at[pick], down_grad.at[0, pick], store_sem.at[1]).start()
-
-    def make_weight_grads():
-        whole = hidden_units // TILE
-        rest = pl.ds(whole * TILE, hidden_units - whole * TILE)
-        for make in (make_up_grad, make_down_grad):
-
-            def body(t, carry, make=make):
-                make(pl.ds(pl.multiple_of(t * TILE, TILE), TILE))
-                return carry
-
-            lax.fori_loop(0, whole, body, 0)
-            make(rest)
+        save_flipped.start()
+
+    def stage_down_grad(c, k):
+        for lo, hi in tiles:
+            down[lo:hi, :] = contract_first(acts[0, :, lo:hi], rows[1]).astype(BF16)
+        save_down.start()
+
+    save_placer = pltpu.make_async_copy(placer, placer_hbm, store_sem.at[0])
+    save_weighted = pltpu.make_async_copy(weighted, weighted_hbm, store_sem.at[1])
+    save_flipped = pltpu.make_async_copy(flipped, flipped_hbm, store_sem.at[2])
+    save_down = pltpu.make_async_copy(down, down_grad.at[0], store_sem.at[3])
+
+    def save_slope(c):
+        return pltpu.make_async_copy(acts.at[1, chunk_rows(c)], slope_hbm.at[chunk_rows(c)], slope_sem.at[c])
 
     stages = {
         "P": make_rows, "A": stage_partial, "B": stage_core, "C": stage_relay, "D": stage_activate,
-        "E": stage_forward, "F": stage_last, "G": stage_result, "X": stage_flip,
+        "E": stage_forward, "F": stage_last, "G": stage_result, "X": stage_flip, "Y": stage_down_grad,
     }
 
+    save_placer.start()
+    save_weighted.start()
     load_tokens.wait()
     load_cotangent.wait()
     pl.semaphore_wait(barrier, n_experts - 1 + 3)
     for step in ORDER:
         stages[step[0]](int(step[1]), int(step[2]))
-    make_weight_grads()
 
     for k in range(2):
         await_sent(sent.at[k, source_rows(1, n_experts - 1)], sent_sem.at[k])
         own_back(k).wait()
+    for save in (save_placer, save_weighted, save_flipped, *map(save_slope, range(len(CHUNKS)))):
+        save.wait()
     quarter = slots // NZ
     await_sent(core_out, core_send.at[0])
     await_sent(first_out, first_send.at[0])
@@ -323,59 +324,67 @@
     for k in range(2):
         await_received(returned.at[k, pl.ds(0, n_experts - 1)], ret_recv.at[k])
         await_sent(results.at[k, source_rows(1, n_experts - 1)], ret_send.at[k])
-    pltpu.make_async_copy(up, up_grad.at[0], store_sem.at[0]).wait()
-    pltpu.make_async_copy(down, down_grad.at[0], store_sem.at[1]).wait()
+    save_down.wait()
 
 
 def combine_kernel(
-    returned_hbm, placer_hbm, weighted_hbm, up_hbm, down_hbm,
+    returned_hbm, placer_hbm, weighted_hbm, flipped_hbm, slope_hbm, down_hbm,
     layer_hbm, token_hbm, up_grad, down_grad,
-    returned, placer, weighted, layer_out, token_grad, up, down, load_sem, out_sem, in_sem, copy_sem,
+    returned, placer, weighted, flipped, slope, layer_out, token_grad, up, down,
+    load_sem, out_sem, in_sem, copy_sem, slope_sem, up_sem,
 ):
     slots, features = placer.shape[0], layer_out.shape[1]
-    first = [
-        pltpu.make_async_copy(weighted_hbm, weighted, load_sem.at[0]),
-        pltpu.make_async_copy(returned_hbm.at[0], returned.at[0], load_sem.at[1]),
+    hidden_units = up.shape[1]
+    tiles = column_tiles(hidden_units)
+    load_flipped = pltpu.make_async_copy(flipped_hbm, flipped, load_sem.at[4])
+    load_slope = [
+        pltpu.make_async_copy(slope_hbm.at[:, lo:hi], slope.at[:, lo:hi], slope_sem.at[index])
+        for index, (lo, hi) in enumerate(tiles)
     ]
-    second = [
-        pltpu.make_async_copy(placer_hbm, placer, load_sem.at[2]),
-        pltpu.make_async_copy(returned_hbm.at[1], returned.at[1], load_sem.at[3]),
+    parts = (
+        (
+            pltpu.make_async_copy(weighted_hbm, weighted, load_sem.at[0]),
+            pltpu.make_async_copy(returned_hbm.at[0], returned.at[0], load_sem.at[1]),
+        ),
+        (
+            pltpu.make_async_copy(placer_hbm, placer, load_sem.at[2]),
+            pltpu.make_async_copy(returned_hbm.at[1], returned.at[1], load_sem.at[3]),
+        ),
+    )
+    size = hidden_units // PIECES
+    picks = [pl.ds(piece * size, size) for piece in range(PIECES)]
+    loads = [
+        pltpu.make_async_copy(down_hbm.at[0, pick], down.at[pick], in_sem.at[piece])
+        for piece, pick in enumerate(picks)
     ]
-    pieces = []
-    for which, (source, between, target) in enumerate(((up_hbm, up, up_grad), (down_hbm, down, down_grad))):
-        size = between.shape[0] // PIECES
-        for piece in range(PIECES):
-            pick = pl.ds(piece * size, size)
-            pieces.append(
-                (
-                    pltpu.make_async_copy(source.at[0, pick], between.at[pick], in_sem.at[which, piece]),
-                    pltpu.make_async_copy(between.at[pick], target.at[0, pick], copy_sem.at[which, piece]),
-                )
-            )
+    stores = [
+        pltpu.make_async_copy(down.at[pick], down_grad.at[0, pick], copy_sem.at[piece])
+        for piece, pick in enumerate(picks)
+    ]
     outs = [
         pltpu.make_async_copy(layer_out, layer_hbm, out_sem.at[0]),
         pltpu.make_async_copy(token_grad, token_hbm, out_sem.at[1]),
     ]
-    for load in (pieces[0][0], *first, pieces[1][0], *second, *(piece[0] for piece in pieces[2:])):
+    up_stores = [
+        pltpu.make_async_copy(up.at[:, lo:hi], up_grad.at[0, :, lo:hi], up_sem.at[index])
+        for index, (lo, hi) in enumerate(tiles)
+    ]
+    for load in (load_flipped, load_slope[0], loads[0], *load_slope[1:], *loads[1:], *parts[0], *parts[1]):
         load.start()
-
-    def pass_on(some):
-        for load, store in some:
+    load_flipped.wait()
+    for index, (lo, hi) in enumerate(tiles):
+        load_slope[index].wait()
+        up[:, lo:hi] = jnp.dot(flipped[...], slope[:, lo:hi], preferred_element_type=F32).astype(BF16)
+        up_stores[index].start()
+        if index < PIECES:
+            loads[index].wait()
+            stores[index].start()
+    for part, picker, result, out, k in zip(parts, (weighted, placer), (layer_out, token_grad), outs, range(2)):
+        for load in part:
             load.wait()
-            store.start()
-
-    pass_on(pieces[:1])
-    for load in first:
-        load.wait()
-    layer_out[...] = contract_first(weighted[...], returned[0].reshape(slots, features)).astype(BF16)
-    outs[0].start()
-    pass_on(pieces[1:2])
-    for load in second:
-        load.wait()
-    token_grad[...] = contract_first(placer[...], returned[1].reshape(slots, features)).astype(BF16)
-    outs[1].start()
-    pass_on(pieces[2:])
-    for copy in (*outs, *(piece[1] for piece in pieces)):
+        result[...] = contract_first(picker[...], returned[k].reshape(slots, features)).astype(BF16)
+        out.start()
+    for copy in (*up_stores, *stores, *outs):
         copy.wait()
 
 
@@ -383,26 +392,29 @@
     n_tok, features = tokens.shape
     hidden_units = up_weight.shape[2]
     slots = NX * NX * CAP
-    vmem = pl.BlockSpec(memory_space=pltpu.VMEM)
     hbm = pl.BlockSpec(memory_space=pl.ANY)
     dma = pltpu.SemaphoreType.DMA
     flops = 12 * slots * features * hidden_units
     n_chunks = len(CHUNKS)
-    returned, up_made, down_made, placer, weighted = pl.pallas_call(
+    n_tiles = len(column_tiles(hidden_units))
+    returned, slope, flipped, down_made, placer, weighted = pl.pallas_call(
         moe_kernel,
         out_shape=(
             jax.ShapeDtypeStruct((2, NX * NX, CAP, features), BF16),
-            jax.ShapeDtypeStruct((1, features, hidden_units), BF16),
+            jax.ShapeDtypeStruct((slots, hidden_units), BF16),
+            jax.ShapeDtypeStruct((features, slots), BF16),
             jax.ShapeDtypeStruct((1, hidden_units, features), BF16),
             jax.ShapeDtypeStruct((slots, n_tok), BF16),
             jax.ShapeDtypeStruct((slots, n_tok), BF16),
         ),
         in_specs=[pl.BlockSpec(memory_space=pltpu.HBM)] * 7,
-        out_specs=(hbm, hbm, hbm, vmem, vmem),
+        out_specs=(hbm,) * 6,
         scratch_shapes=[
             pltpu.VMEM((features, hidden_units), BF16),
             pltpu.VMEM((hidden_units, features), BF16),
             pltpu.VMEM((features, slots), BF16),
+            pltpu.VMEM((slots, n_tok), BF16),
+            pltpu.VMEM((slots, n_tok), BF16),
             pltpu.VMEM((n_tok, features), BF16),
             pltpu.VMEM((n_tok, features), BF16),
             pltpu.VMEM((2, n_tok), jnp.int32),
@@ -437,7 +449,8 @@
             dma((n_chunks, 2)),
             dma((2,)),
             dma((2,)),
-            dma((2,)),
+            dma((4,)),
+            dma((n_chunks,)),
         ],
         compiler_params=pltpu.CompilerParams(
             collective_id=0, has_side_effects=True, vmem_limit_bytes=VMEM_LIMIT
@@ -455,27 +468,31 @@
             jax.ShapeDtypeStruct((1, features, hidden_units), BF16),
             jax.ShapeDtypeStruct((1, hidden_units, features), BF16),
         ),
-        in_specs=[hbm] * 5,
+        in_specs=[hbm] * 6,
         out_specs=(hbm,) * 4,
         scratch_shapes=[
             pltpu.VMEM((2, NX * NX, CAP, features), BF16),
             pltpu.VMEM((slots, n_tok), BF16),
             pltpu.VMEM((slots, n_tok), BF16),
+            pltpu.VMEM((features, slots), BF16),
+            pltpu.VMEM((slots, hidden_units), BF16),
             pltpu.VMEM((n_tok, features), BF16),
             pltpu.VMEM((n_tok, features), BF16),
             pltpu.VMEM((features, hidden_units), BF16),
             pltpu.VMEM((hidden_units, features), BF16),
-            dma((4,)),
+            dma((5,)),
             dma((2,)),
-            dma((2, PIECES)),
-            dma((2, PIECES)),
+            dma((PIECES,)),
+            dma((PIECES,)),
+            dma((n_tiles,)),
+            dma((n_tiles,)),
         ],
         compiler_params=pltpu.CompilerParams(vmem_limit_bytes=COMBINE_VMEM_LIMIT),
         cost_estimate=pl.CostEstimate(
             flops=4 * slots * n_tok * features, bytes_accessed=8 * features * hidden_units, transcendentals=0
         ),
         name="combine",
-    )(returned, placer, weighted, up_made, down_made)
+    )(returned, placer, weighted, flipped, slope, down_made)
 
 
 def solution(mesh):

time: 93.2 us -> 92.5 us (level)
  Pallas kernels: 92.3 us -> 90.8 us
    pallas_call x1, Pallas kernels: 84.9 us -> 83.3 us  [per_device(): pl.pallas_call(moe_kernel, out_shape=(jax.ShapeDtypeStruct((2, NX * NX, C...]
where the time goes in v4:
time: 92.5 us; the launch traced here: 91.6 us
  Pallas kernels  90.8 us (98%)
    pallas_call x1, Pallas kernels, per_device(): pl.pallas_call(moe_kernel, out_shape=(jax.ShapeDtypeStruct((2, NX * NX, C...  83.3 us
    pallas_call x1, Pallas kernels, per_device(): pl.pallas_call(combine_kernel, out_shape=(jax.ShapeDtypeStruct((n_tok, fe...  7.5 us

profile of v4, /device:TPU:1, one launch (start us, length us, event | category | flops | bytes accessed | tf_op | source)
XLA Modules:
  0.0 91.6 jit_solution(9004729581832978581)
XLA Ops:
  0.6 83.3 %moe_exchange.1 = (bf16[2,16,32,896]{3,2,1,0:T(8,128)(2,1)}, bf16[512,2432]{1,0:T(8,128)(2,1)}, bf16[896,512]{1,0:T(8,128)(2,1)}, bf16[1,2432,896]{2,1,0:T(8,128...) custom-call(bf16[128,896]{1,0:T(8,128)(2,1)} %tokens_hbm.1, bf16[128,896]{1,0:T(8,128)(2,1)} %cotangent_hbm.1, ...), custom_call_target="tpu_custom_call" | custom-call | flops 13388218368 | bytes 8716288 | tf_op jit(solution)/shard_map/moe_exchange/pallas_call | solution.py:400
  84.0 7.5 %combine.1 = (bf16[128,896]{1,0:T(8,128)(2,1)}, bf16[128,896]{1,0:T(8,128)(2,1)}, bf16[1,896,2432]{2,1,0:T(8,128)(2,1)}, bf16[1,2432,896]{2,1,0:T(8,128)(2,1)}) custom-call(bf16[2,16,32,896]{3,2,1,0:T(8,128)(2,1)} %get-tuple-element.10.returned_hbm, bf16[512,128]{1,0:T(8,128)(2,1)} %get-tuple-element.11.placer_hbm, ...), custom_call_target="tpu_custom_call" | custom-call | flops 234881024 | bytes 17432576 | tf_op jit(solution)/shard_map/combine/pallas_call | solution.py:463

commit v5 on v4

--- a/solution.py
+++ b/solution.py
@@ -14,13 +14,14 @@
 NZ = 4
 CAP = 32
 SOURCES = tuple((s % NX, (s + s // NX) % NX) for s in range(NX * NX))
-CHUNKS = ((0, 4), (4, 12), (12, 16))
+CHUNKS = ((0, 4), (4, 8), (8, 12), (12, 16))
 ORDER = (
-    "P01", "P00", "P10", "A01", "A00", "P11", "B01", "A10", "B00", "B10", "C00", "C01",
-    "A11", "C10", "P21", "B11", "D10", "C11", "P20", "D00", "E10", "A20", "B20", "D11",
-    "F10", "D01", "A21", "G10", "C20", "E11", "B21", "D20", "F11", "E01", "C21", "E00",
-    "G11", "E20", "F01", "D21", "F20", "X00", "F00", "G01", "E21", "G20", "F21", "G00",
-    "Y00", "G21",
+    "P10", "P00", "P01", "P11", "A10", "P20", "A00", "B10", "A01", "B00", "B01", "A11",
+    "C10", "C00", "B11", "P30", "C01", "D10", "P31", "C11", "D00", "A20", "D01", "P21",
+    "B20", "D11", "E10", "E01", "A30", "E00", "C20", "A21", "B30", "E11", "A31", "B21",
+    "C30", "F01", "F00", "B31", "D20", "F10", "F11", "G00", "C31", "D30", "G10", "E20",
+    "C21", "D31", "G11", "E30", "F20", "D21", "G01", "E31", "F30", "X00", "G20", "E21",
+    "F31", "G30", "G31", "F21", "G21", "Y00",
 )
 TILE = 512
 PIECES = 4
@@ -159,14 +160,21 @@
         lo, hi = CHUNKS[c]
         return range(max(lo, 1), hi)
 
+    dispatch_order = [(int(step[1]), int(step[2])) for step in ORDER if step[0] == "P"]
+
     def make_rows(c, k):
         matrix, picker = ((tokens, placer), (cotangent, weighted))[k]
+        is_first = (c, k) == next((at, kind) for at, kind in dispatch_order if kind == k)
+        if is_first:
+            (load_tokens, load_cotangent)[k].wait()
         picked = [picker[pl.ds(pl.multiple_of(owners[s] * CAP, CAP), CAP), :] for s in range(*CHUNKS[c])]
         sent[k, chunk_rows(c), :] = jnp.dot(
             jnp.concatenate(picked, axis=0), matrix[...], preferred_element_type=F32
         ).astype(BF16)
         if c == 0:
             own_rows(k).start()
+        if (c, k) == dispatch_order[0]:
+            pl.semaphore_wait(barrier, n_experts - 1 + 3)
         for s in remote_sources(c):
             remote(
                 sent.at[k, source_rows(s)], rows.at[k, source_rows(s)], sent_sem.at[k], rows_sem.at[c, k],
@@ -303,9 +311,6 @@
 
     save_placer.start()
     save_weighted.start()
-    load_tokens.wait()
-    load_cotangent.wait()
-    pl.semaphore_wait(barrier, n_experts - 1 + 3)
     for step in ORDER:
         stages[step[0]](int(step[1]), int(step[2]))
 

time: 92.5 us -> 87.1 us (0.942)
  Pallas kernels: 90.8 us -> 86.2 us
    pallas_call x1, Pallas kernels: 83.3 us -> 78.7 us  [per_device(): pl.pallas_call(moe_kernel, out_shape=(jax.ShapeDtypeStruct((2, NX * NX, C...]
where the time goes in v5:
time: 87.1 us; the launch traced here: 87 us
  Pallas kernels  86.2 us (99%)
    pallas_call x1, Pallas kernels, per_device(): pl.pallas_call(moe_kernel, out_shape=(jax.ShapeDtypeStruct((2, NX * NX, C...  78.7 us
    pallas_call x1, Pallas kernels, per_device(): pl.pallas_call(combine_kernel, out_shape=(jax.ShapeDtypeStruct((n_tok, fe...  7.49 us

profile of v5, /device:TPU:1, one launch (start us, length us, event | category | flops | bytes accessed | tf_op | source)
XLA Modules:
  0.0 87.0 jit_solution(13273612151428147180)
XLA Ops:
  0.6 78.7 %moe_exchange.1 = (bf16[2,16,32,896]{3,2,1,0:T(8,128)(2,1)}, bf16[512,2432]{1,0:T(8,128)(2,1)}, bf16[896,512]{1,0:T(8,128)(2,1)}, bf16[1,2432,896]{2,1,0:T(8,128...) custom-call(bf16[128,896]{1,0:T(8,128)(2,1)} %tokens_hbm.1, bf16[128,896]{1,0:T(8,128)(2,1)} %cotangent_hbm.1, ...), custom_call_target="tpu_custom_call" | custom-call | flops 13388218368 | bytes 8716288 | tf_op jit(solution)/shard_map/moe_exchange/pallas_call | solution.py:405
  79.4 7.5 %combine.1 = (bf16[128,896]{1,0:T(8,128)(2,1)}, bf16[128,896]{1,0:T(8,128)(2,1)}, bf16[1,896,2432]{2,1,0:T(8,128)(2,1)}, bf16[1,2432,896]{2,1,0:T(8,128)(2,1)}) custom-call(bf16[2,16,32,896]{3,2,1,0:T(8,128)(2,1)} %get-tuple-element.10.returned_hbm, bf16[512,128]{1,0:T(8,128)(2,1)} %get-tuple-element.11.placer_hbm, ...), custom_call_target="tpu_custom_call" | custom-call | flops 234881024 | bytes 17432576 | tf_op jit(solution)/shard_map/combine/pallas_call | solution.py:468

commit v6 on v5

--- a/solution.py
+++ b/solution.py
@@ -13,7 +13,12 @@
 NX = 4
 NZ = 4
 CAP = 32
-SOURCES = tuple((s % NX, (s + s // NX) % NX) for s in range(NX * NX))
+SOURCES = (
+    (0, 0), (2, 0), (0, 2), (2, 2),
+    (1, 0), (3, 0), (0, 1), (0, 3),
+    (1, 1), (3, 3), (1, 3), (3, 1),
+    (2, 1), (1, 2), (2, 3), (3, 2),
+)
 CHUNKS = ((0, 4), (4, 8), (8, 12), (12, 16))
 ORDER = (
     "P10", "P00", "P01", "P11", "A10", "P20", "A00", "B10", "A01", "B00", "B01", "A11",
@@ -121,18 +126,19 @@
     )
     limit = jnp.sum(jnp.where(diagonal, plan[...].astype(F32), 0.0), axis=1, keepdims=True)
     slot_id = lax.broadcasted_iota(jnp.int32, (slots, n_tok), 0).astype(F32)
-    ones = jnp.zeros((slots, n_tok), F32)
-    scaled = jnp.zeros((slots, n_tok), F32)
+    hits = []
     pairs = ((first, named_first, earlier), (second, named_second, earlier + named_first))
-    for k, (named_id, named, count) in enumerate(pairs):
+    for named_id, named, count in pairs:
         position = jnp.sum(count * named, axis=0, keepdims=True)
         allowed = jnp.sum(limit * named, axis=0, keepdims=True)
-        slot = jnp.where(position < allowed, named_id.astype(F32) * CAP + position, -1.0)
-        hit = slot_id == slot
-        ones = ones + jnp.where(hit, 1.0, 0.0)
-        scaled = scaled + jnp.where(hit, route_weights[k : k + 1, :].astype(F32), 0.0)
-    placer[...] = ones.astype(BF16)
-    weighted[...] = scaled.astype(BF16)
+        hits.append(slot_id == jnp.where(position < allowed, named_id.astype(F32) * CAP + position, -1.0))
+    placer[...] = jnp.where(hits[0], 1.0, jnp.where(hits[1], 1.0, 0.0)).astype(BF16)
+
+    def make_weighted():
+        scales = [route_weights[k : k + 1, :].astype(F32) for k in range(2)]
+        weighted[...] = jnp.where(hits[0], scales[0], jnp.where(hits[1], scales[1], 0.0)).astype(BF16)
+        save_placer.start()
+        save_weighted.start()
 
     def source_rows(s, count=1):
         return pl.ds(s * CAP, count * CAP)
@@ -167,6 +173,8 @@
         is_first = (c, k) == next((at, kind) for at, kind in dispatch_order if kind == k)
         if is_first:
             (load_tokens, load_cotangent)[k].wait()
+            if k == 1:
+                make_weighted()
         picked = [picker[pl.ds(pl.multiple_of(owners[s] * CAP, CAP), CAP), :] for s in range(*CHUNKS[c])]
         sent[k, chunk_rows(c), :] = jnp.dot(
             jnp.concatenate(picked, axis=0), matrix[...], preferred_element_type=F32
@@ -309,8 +317,6 @@
         "E": stage_forward, "F": stage_last, "G": stage_result, "X": stage_flip, "Y": stage_down_grad,
     }
 
-    save_placer.start()
-    save_weighted.start()
     for step in ORDER:
         stages[step[0]](int(step[1]), int(step[2]))
 

time: 87.1 us -> 85.6 us (0.983)
  Pallas kernels: 86.2 us -> 84.7 us
    pallas_call x1, Pallas kernels: 78.7 us -> 77.2 us  [per_device(): pl.pallas_call(moe_kernel, out_shape=(jax.ShapeDtypeStruct((2, NX * NX, C...]
where the time goes in v6:
time: 85.6 us; the launch traced here: 85.5 us
  Pallas kernels  84.7 us (99%)
    pallas_call x1, Pallas kernels, per_device(): pl.pallas_call(moe_kernel, out_shape=(jax.ShapeDtypeStruct((2, NX * NX, C...  77.2 us
    pallas_call x1, Pallas kernels, per_device(): pl.pallas_call(combine_kernel, out_shape=(jax.ShapeDtypeStruct((n_tok, fe...  7.49 us

profile of v6, /device:TPU:1, one launch (start us, length us, event | category | flops | bytes accessed | tf_op | source)
XLA Modules:
  0.0 85.5 jit_solution(5079755356721344489)
XLA Ops:
  0.6 77.2 %moe_exchange.1 = (bf16[2,16,32,896]{3,2,1,0:T(8,128)(2,1)}, bf16[512,2432]{1,0:T(8,128)(2,1)}, bf16[896,512]{1,0:T(8,128)(2,1)}, bf16[1,2432,896]{2,1,0:T(8,128...) custom-call(bf16[128,896]{1,0:T(8,128)(2,1)} %tokens_hbm.1, bf16[128,896]{1,0:T(8,128)(2,1)} %cotangent_hbm.1, ...), custom_call_target="tpu_custom_call" | custom-call | flops 13388218368 | bytes 8716288 | tf_op jit(solution)/shard_map/moe_exchange/pallas_call | solution.py:411
  77.8 7.5 %combine.1 = (bf16[128,896]{1,0:T(8,128)(2,1)}, bf16[128,896]{1,0:T(8,128)(2,1)}, bf16[1,896,2432]{2,1,0:T(8,128)(2,1)}, bf16[1,2432,896]{2,1,0:T(8,128)(2,1)}) custom-call(bf16[2,16,32,896]{3,2,1,0:T(8,128)(2,1)} %get-tuple-element.10.returned_hbm, bf16[512,128]{1,0:T(8,128)(2,1)} %get-tuple-element.11.placer_hbm, ...), custom_call_target="tpu_custom_call" | custom-call | flops 234881024 | bytes 17432576 | tf_op jit(solution)/shard_map/combine/pallas_call | solution.py:474

commit v7 on v6

--- a/solution.py
+++ b/solution.py
@@ -21,12 +21,12 @@
 )
 CHUNKS = ((0, 4), (4, 8), (8, 12), (12, 16))
 ORDER = (
-    "P10", "P00", "P01", "P11", "A10", "P20", "A00", "B10", "A01", "B00", "B01", "A11",
-    "C10", "C00", "B11", "P30", "C01", "D10", "P31", "C11", "D00", "A20", "D01", "P21",
-    "B20", "D11", "E10", "E01", "A30", "E00", "C20", "A21", "B30", "E11", "A31", "B21",
-    "C30", "F01", "F00", "B31", "D20", "F10", "F11", "G00", "C31", "D30", "G10", "E20",
-    "C21", "D31", "G11", "E30", "F20", "D21", "G01", "E31", "F30", "X00", "G20", "E21",
-    "F31", "G30", "G31", "F21", "G21", "Y00",
+    "P10", "P11", "P00", "P01", "A10", "A11", "P20", "B11", "B10", "A00", "P21", "C11",
+    "A01", "B00", "C10", "B01", "A20", "C00", "P30", "B20", "D10", "A21", "D00", "P31",
+    "C01", "C20", "D11", "E00", "E10", "B21", "D01", "A30", "F10", "D20", "A31", "F00",
+    "B30", "E01", "B31", "G10", "C30", "E20", "E11", "C31", "G00", "F01", "D30", "F20",
+    "C21", "F11", "G01", "D31", "G11", "E30", "D21", "G20", "E31", "X00", "F30", "G30",
+    "F31", "E21", "G31", "F21", "G21", "Y00",
 )
 TILE = 512
 PIECES = 4
@@ -103,7 +103,7 @@
             ((routes_hbm, routes), (weights_hbm, route_weights), (plan_hbm, plan))
         )
     ]
-    for load in (*load_routing, load_tokens, load_cotangent, load_up, load_down):
+    for load in (*load_routing, load_tokens):
         load.start()
     for peer in sources[1:]:
         pl.semaphore_signal(barrier, inc=1, device_id={"expert": peer, "tensor": place}, device_id_type=MESH)
@@ -188,6 +188,9 @@
                 sent.at[k, source_rows(s)], rows.at[k, source_rows(s)], sent_sem.at[k], rows_sem.at[c, k],
                 {"expert": owners[s], "tensor": place},
             ).start()
+        if (c, k) == dispatch_order[0]:
+            for load in (load_cotangent, load_up, load_down):
+                load.start()
 
     def own_rows(k):
         return pltpu.make_async_copy(sent.at[k, source_rows(0)], rows.at[k, source_rows(0)], own_sem.at[0, k])
@@ -380,11 +383,14 @@
         pltpu.make_async_copy(up.at[:, lo:hi], up_grad.at[0, :, lo:hi], up_sem.at[index])
         for index, (lo, hi) in enumerate(tiles)
     ]
-    for load in (load_flipped, load_slope[0], loads[0], *load_slope[1:], *loads[1:], *parts[0], *parts[1]):
+    for load in (load_flipped, *load_slope[:2]):
         load.start()
     load_flipped.wait()
     for index, (lo, hi) in enumerate(tiles):
         load_slope[index].wait()
+        if index == 0:
+            for load in (loads[0], *load_slope[2:], *loads[1:], *parts[0], *parts[1]):
+                load.start()
         up[:, lo:hi] = jnp.dot(flipped[...], slope[:, lo:hi], preferred_element_type=F32).astype(BF16)
         up_stores[index].start()
         if index < PIECES:

time: 85.6 us -> 84 us (0.981)
  Pallas kernels: 84.7 us -> 83.1 us
    pallas_call x1, Pallas kernels: 77.2 us -> 75.4 us  [per_device(): pl.pallas_call(moe_kernel, out_shape=(jax.ShapeDtypeStruct((2, NX * NX, C...]
where the time goes in v7:
time: 84 us; the launch traced here: 83.9 us
  Pallas kernels  83.1 us (99%)
    pallas_call x1, Pallas kernels, per_device(): pl.pallas_call(moe_kernel, out_shape=(jax.ShapeDtypeStruct((2, NX * NX, C...  75.4 us
    pallas_call x1, Pallas kernels, per_device(): pl.pallas_call(combine_kernel, out_shape=(jax.ShapeDtypeStruct((n_tok, fe...  7.68 us

profile of v7, /device:TPU:1, one launch (start us, length us, event | category | flops | bytes accessed | tf_op | source)
XLA Modules:
  0.0 83.9 jit_solution(1219314326803845135)
XLA Ops:
  0.6 75.4 %moe_exchange.1 = (bf16[2,16,32,896]{3,2,1,0:T(8,128)(2,1)}, bf16[512,2432]{1,0:T(8,128)(2,1)}, bf16[896,512]{1,0:T(8,128)(2,1)}, bf16[1,2432,896]{2,1,0:T(8,128...) custom-call(bf16[128,896]{1,0:T(8,128)(2,1)} %tokens_hbm.1, bf16[128,896]{1,0:T(8,128)(2,1)} %cotangent_hbm.1, ...), custom_call_target="tpu_custom_call" | custom-call | flops 13388218368 | bytes 8716288 | tf_op jit(solution)/shard_map/moe_exchange/pallas_call | solution.py:417
  76.0 7.7 %combine.1 = (bf16[128,896]{1,0:T(8,128)(2,1)}, bf16[128,896]{1,0:T(8,128)(2,1)}, bf16[1,896,2432]{2,1,0:T(8,128)(2,1)}, bf16[1,2432,896]{2,1,0:T(8,128)(2,1)}) custom-call(bf16[2,16,32,896]{3,2,1,0:T(8,128)(2,1)} %get-tuple-element.10.returned_hbm, bf16[512,128]{1,0:T(8,128)(2,1)} %get-tuple-element.11.placer_hbm, ...), custom_call_target="tpu_custom_call" | custom-call | flops 234881024 | bytes 17432576 | tf_op jit(solution)/shard_map/combine/pallas_call | solution.py:480

commit v8 on v7

--- a/solution.py
+++ b/solution.py
@@ -30,8 +30,9 @@
 )
 TILE = 512
 PIECES = 4
-VMEM_LIMIT = 60 * 1024 * 1024
-COMBINE_VMEM_LIMIT = 60 * 1024 * 1024
+ROUTE_VMEM_LIMIT = 60 * 1024 * 1024
+VMEM_LIMIT = 41 * 1024 * 1024
+COMBINE_VMEM_LIMIT = 28 * 1024 * 1024
 
 
 def contract_last(left, right):
@@ -50,67 +51,25 @@
     return lax.rem(value + size, size)
 
 
-def moe_kernel(
-    tokens_hbm, cotangent_hbm, routes_hbm, weights_hbm, plan_hbm, up_hbm, down_hbm,
-    returned, slope_hbm, flipped_hbm, down_grad, placer_hbm, weighted_hbm,
-    up, down, flipped, placer, weighted, tokens, cotangent, routes, route_weights, plan, sent, rows, part, core_out, core_in,
-    first_out, first_in, second_out, second_in, acts, results,
-    load_sem, own_sem, sent_sem, rows_sem, core_send, core_recv,
-    first_send, first_recv, second_send, second_recv,
-    near_send, near_recv, far_send, far_recv, mate_send, mate_recv,
-    ret_send, ret_recv, store_sem, slope_sem,
+def route_kernel(
+    tokens_hbm, cotangent_hbm, routes_hbm, weights_hbm, plan_hbm,
+    sent_hbm, placer_hbm, weighted_hbm,
+    tokens, cotangent, routes, route_weights, plan, placer, weighted, sent, load_sem, store_sem,
 ):
-    expert = lax.axis_index("expert")
-    place = lax.axis_index("tensor")
-    x, y = lax.div(expert, NX), lax.rem(expert, NX)
-    z, core = lax.div(place, 2), lax.rem(place, 2)
-    z_next, z_prev, z_far = wrap(z + 1, NZ), wrap(z - 1, NZ), wrap(z + 2, NZ)
-    other = 1 - core
     n_tok, features = tokens.shape
-    hidden_units = up.shape[1]
-    split = ((hidden_units // 128 + 1) // 2) * 128
-    tiles = column_tiles(hidden_units)
-    half_a, half_b = pl.ds(0, split), pl.ds(split, hidden_units - split)
     n_experts, slots = NX * NX, NX * NX * CAP
-
-    def at_z(which):
-        return {"expert": expert, "tensor": which * 2 + core}
-
-    next_chip, prev_chip = at_z(z_next), at_z(z_prev)
-    mate = {"expert": expert, "tensor": z * 2 + other}
-    owners = [wrap(x - dx, NX) * NX + wrap(y - dy, NX) for dx, dy in SOURCES]
-    sources = [wrap(x + dx, NX) * NX + wrap(y + dy, NX) for dx, dy in SOURCES]
-
-    def remote(src, dst, send, recv, device):
-        return pltpu.make_async_remote_copy(
-            src_ref=src, dst_ref=dst, send_sem=send, recv_sem=recv, device_id=device, device_id_type=MESH
+    loads = [
+        pltpu.make_async_copy(source, target, load_sem.at[which])
+        for which, (source, target) in enumerate(
+            (
+                (routes_hbm, routes), (weights_hbm, route_weights), (plan_hbm, plan),
+                (tokens_hbm, tokens), (cotangent_hbm, cotangent),
+            )
         )
-
-    def await_received(ref, sem):
-        remote(ref, ref, sem, sem, mate).wait_recv()
-
-    def await_sent(ref, sem):
-        remote(ref, ref, sem, sem, mate).wait_send()
-
-    barrier = pltpu.get_barrier_semaphore()
-    load_tokens = pltpu.make_async_copy(tokens_hbm, tokens, load_sem.at[2])
-    load_cotangent = pltpu.make_async_copy(cotangent_hbm, cotangent, load_sem.at[3])
-    load_up = pltpu.make_async_copy(up_hbm.at[0], up, load_sem.at[0])
-    load_down = pltpu.make_async_copy(down_hbm.at[0], down, load_sem.at[1])
-    load_routing = [
-        pltpu.make_async_copy(source, target, load_sem.at[4 + which])
-        for which, (source, target) in enumerate(
-            ((routes_hbm, routes), (weights_hbm, route_weights), (plan_hbm, plan))
-        )
-    ]
-    for load in (*load_routing, load_tokens):
+    ]
+    for load in loads:
         load.start()
-    for peer in sources[1:]:
-        pl.semaphore_signal(barrier, inc=1, device_id={"expert": peer, "tensor": place}, device_id_type=MESH)
-    for device in (next_chip, prev_chip, mate):
-        pl.semaphore_signal(barrier, inc=1, device_id=device, device_id_type=MESH)
-
-    for load in load_routing:
+    for load in loads[:3]:
         load.wait()
 
     expert_id = lax.broadcasted_iota(jnp.int32, (n_experts, n_tok), 0)
@@ -134,11 +93,71 @@
         hits.append(slot_id == jnp.where(position < allowed, named_id.astype(F32) * CAP + position, -1.0))
     placer[...] = jnp.where(hits[0], 1.0, jnp.where(hits[1], 1.0, 0.0)).astype(BF16)
 
-    def make_weighted():
-        scales = [route_weights[k : k + 1, :].astype(F32) for k in range(2)]
-        weighted[...] = jnp.where(hits[0], scales[0], jnp.where(hits[1], scales[1], 0.0)).astype(BF16)
-        save_placer.start()
-        save_weighted.start()
+    scales = [route_weights[k : k + 1, :].astype(F32) for k in range(2)]
+    weighted[...] = jnp.where(hits[0], scales[0], jnp.where(hits[1], scales[1], 0.0)).astype(BF16)
+    stores = [
+        pltpu.make_async_copy(placer, placer_hbm, store_sem.at[0]),
+        pltpu.make_async_copy(weighted, weighted_hbm, store_sem.at[1]),
+    ]
+    for store in stores:
+        store.start()
+    for k, (matrix, picker) in enumerate(((tokens, placer), (cotangent, weighted))):
+        loads[3 + k].wait()
+        sent[k] = jnp.dot(picker[...], matrix[...], preferred_element_type=F32).astype(BF16)
+        stores.append(pltpu.make_async_copy(sent.at[k], sent_hbm.at[k], store_sem.at[2 + k]))
+        stores[-1].start()
+    for store in stores:
+        store.wait()
+
+
+def moe_kernel(
+    sent, up_hbm, down_hbm,
+    returned, slope_hbm, flipped_hbm, down_grad,
+    up, down, flipped, rows, part, core_out, core_in,
+    first_out, first_in, second_out, second_in, acts, results,
+    load_sem, own_sem, sent_sem, rows_sem, core_send, core_recv,
+    first_send, first_recv, second_send, second_recv,
+    near_send, near_recv, far_send, far_recv, mate_send, mate_recv,
+    ret_send, ret_recv, store_sem, slope_sem,
+):
+    expert = lax.axis_index("expert")
+    place = lax.axis_index("tensor")
+    x, y = lax.div(expert, NX), lax.rem(expert, NX)
+    z, core = lax.div(place, 2), lax.rem(place, 2)
+    z_next, z_prev, z_far = wrap(z + 1, NZ), wrap(z - 1, NZ), wrap(z + 2, NZ)
+    other = 1 - core
+    features, hidden_units = up.shape
+    split = ((hidden_units // 128 + 1) // 2) * 128
+    tiles = column_tiles(hidden_units)
+    half_a, half_b = pl.ds(0, split), pl.ds(split, hidden_units - split)
+    n_experts, slots = NX * NX, NX * NX * CAP
+
+    def at_z(which):
+        return {"expert": expert, "tensor": which * 2 + core}
+
+    next_chip, prev_chip = at_z(z_next), at_z(z_prev)
+    mate = {"expert": expert, "tensor": z * 2 + other}
+    owners = [wrap(x - dx, NX) * NX + wrap(y - dy, NX) for dx, dy in SOURCES]
+    sources = [wrap(x + dx, NX) * NX + wrap(y + dy, NX) for dx, dy in SOURCES]
+
+    def remote(src, dst, send, recv, device):
+        return pltpu.make_async_remote_copy(
+            src_ref=src, dst_ref=dst, send_sem=send, recv_sem=recv, device_id=device, device_id_type=MESH
+        )
+
+    def await_received(ref, sem):
+        remote(ref, ref, sem, sem, mate).wait_recv()
+
+    def await_sent(ref, sem):
+        remote(ref, ref, sem, sem, mate).wait_send()
+
+    barrier = pltpu.get_barrier_semaphore()
+    load_up = pltpu.make_async_copy(up_hbm.at[0], up, load_sem.at[0])
+    load_down = pltpu.make_async_copy(down_hbm.at[0], down, load_sem.at[1])
+    for peer in sources[1:]:
+        pl.semaphore_signal(barrier, inc=1, device_id={"expert": peer, "tensor": place}, device_id_type=MESH)
+    for device in (next_chip, prev_chip, mate):
+        pl.semaphore_signal(barrier, inc=1, device_id=device, device_id_type=MESH)
 
     def source_rows(s, count=1):
         return pl.ds(s * CAP, count * CAP)
@@ -168,32 +187,25 @@
 
     dispatch_order = [(int(step[1]), int(step[2])) for step in ORDER if step[0] == "P"]
 
-    def make_rows(c, k):
-        matrix, picker = ((tokens, placer), (cotangent, weighted))[k]
-        is_first = (c, k) == next((at, kind) for at, kind in dispatch_order if kind == k)
-        if is_first:
-            (load_tokens, load_cotangent)[k].wait()
-            if k == 1:
-                make_weighted()
-        picked = [picker[pl.ds(pl.multiple_of(owners[s] * CAP, CAP), CAP), :] for s in range(*CHUNKS[c])]
-        sent[k, chunk_rows(c), :] = jnp.dot(
-            jnp.concatenate(picked, axis=0), matrix[...], preferred_element_type=F32
-        ).astype(BF16)
+    def expert_rows(which):
+        return pl.ds(pl.multiple_of(which * CAP, CAP), CAP)
+
+    def stage_dispatch(c, k):
+        if (c, k) == dispatch_order[0]:
+            pl.semaphore_wait(barrier, n_experts - 1 + 3)
         if c == 0:
             own_rows(k).start()
-        if (c, k) == dispatch_order[0]:
-            pl.semaphore_wait(barrier, n_experts - 1 + 3)
         for s in remote_sources(c):
             remote(
-                sent.at[k, source_rows(s)], rows.at[k, source_rows(s)], sent_sem.at[k], rows_sem.at[c, k],
+                sent.at[k, expert_rows(owners[s])], rows.at[k, source_rows(s)], sent_sem.at[k], rows_sem.at[c, k],
                 {"expert": owners[s], "tensor": place},
             ).start()
         if (c, k) == dispatch_order[0]:
-            for load in (load_cotangent, load_up, load_down):
-                load.start()
+            load_up.start()
+            load_down.start()
 
     def own_rows(k):
-        return pltpu.make_async_copy(sent.at[k, source_rows(0)], rows.at[k, source_rows(0)], own_sem.at[0, k])
+        return pltpu.make_async_copy(sent.at[k, expert_rows(expert)], rows.at[k, source_rows(0)], own_sem.at[0, k])
 
     def own_back(k):
         return pltpu.make_async_copy(results.at[k, source_rows(0)], returned.at[k, expert], own_sem.at[1, k])
@@ -307,16 +319,14 @@
             down[lo:hi, :] = contract_first(acts[0, :, lo:hi], rows[1]).astype(BF16)
         save_down.start()
 
-    save_placer = pltpu.make_async_copy(placer, placer_hbm, store_sem.at[0])
-    save_weighted = pltpu.make_async_copy(weighted, weighted_hbm, store_sem.at[1])
-    save_flipped = pltpu.make_async_copy(flipped, flipped_hbm, store_sem.at[2])
-    save_down = pltpu.make_async_copy(down, down_grad.at[0], store_sem.at[3])
+    save_flipped = pltpu.make_async_copy(flipped, flipped_hbm, store_sem.at[0])
+    save_down = pltpu.make_async_copy(down, down_grad.at[0], store_sem.at[1])
 
     def save_slope(c):
         return pltpu.make_async_copy(acts.at[1, chunk_rows(c)], slope_hbm.at[chunk_rows(c)], slope_sem.at[c])
 
     stages = {
-        "P": make_rows, "A": stage_partial, "B": stage_core, "C": stage_relay, "D": stage_activate,
+        "P": stage_dispatch, "A": stage_partial, "B": stage_core, "C": stage_relay, "D": stage_activate,
         "E": stage_forward, "F": stage_last, "G": stage_result, "X": stage_flip, "Y": stage_down_grad,
     }
 
@@ -326,7 +336,7 @@
     for k in range(2):
         await_sent(sent.at[k, source_rows(1, n_experts - 1)], sent_sem.at[k])
         own_back(k).wait()
-    for save in (save_placer, save_weighted, save_flipped, *map(save_slope, range(len(CHUNKS)))):
+    for save in (save_flipped, *map(save_slope, range(len(CHUNKS)))):
         save.wait()
     quarter = slots // NZ
     await_sent(core_out, core_send.at[0])
@@ -414,30 +424,47 @@
     flops = 12 * slots * features * hidden_units
     n_chunks = len(CHUNKS)
     n_tiles = len(column_tiles(hidden_units))
-    returned, slope, flipped, down_made, placer, weighted = pl.pallas_call(
+    sent, placer, weighted = pl.pallas_call(
+        route_kernel,
+        out_shape=(
+            jax.ShapeDtypeStruct((2, slots, features), BF16),
+            jax.ShapeDtypeStruct((slots, n_tok), BF16),
+            jax.ShapeDtypeStruct((slots, n_tok), BF16),
+        ),
+        in_specs=[hbm] * 5,
+        out_specs=(hbm,) * 3,
+        scratch_shapes=[
+            pltpu.VMEM((n_tok, features), BF16),
+            pltpu.VMEM((n_tok, features), BF16),
+            pltpu.VMEM((2, n_tok), jnp.int32),
+            pltpu.VMEM((2, n_tok), BF16),
+            pltpu.VMEM((1, NX * NX), jnp.int32),
+            pltpu.VMEM((slots, n_tok), BF16),
+            pltpu.VMEM((slots, n_tok), BF16),
+            pltpu.VMEM((2, slots, features), BF16),
+            dma((5,)),
+            dma((4,)),
+        ],
+        compiler_params=pltpu.CompilerParams(vmem_limit_bytes=ROUTE_VMEM_LIMIT),
+        cost_estimate=pl.CostEstimate(
+            flops=4 * slots * n_tok * features, bytes_accessed=6 * slots * features, transcendentals=0
+        ),
+        name="route",
+    )(tokens, cotangent, routes.T, route_weights.T, capacity_plan[None])
+    returned, slope, flipped, down_made = pl.pallas_call(
         moe_kernel,
         out_shape=(
             jax.ShapeDtypeStruct((2, NX * NX, CAP, features), BF16),
             jax.ShapeDtypeStruct((slots, hidden_units), BF16),
             jax.ShapeDtypeStruct((features, slots), BF16),
             jax.ShapeDtypeStruct((1, hidden_units, features), BF16),
-            jax.ShapeDtypeStruct((slots, n_tok), BF16),
-            jax.ShapeDtypeStruct((slots, n_tok), BF16),
-        ),
-        in_specs=[pl.BlockSpec(memory_space=pltpu.HBM)] * 7,
-        out_specs=(hbm,) * 6,
+        ),
+        in_specs=[hbm] * 3,
+        out_specs=(hbm,) * 4,
         scratch_shapes=[
             pltpu.VMEM((features, hidden_units), BF16),
             pltpu.VMEM((hidden_units, features), BF16),
             pltpu.VMEM((features, slots), BF16),
-            pltpu.VMEM((slots, n_tok), BF16),
-            pltpu.VMEM((slots, n_tok), BF16),
-            pltpu.VMEM((n_tok, features), BF16),
-            pltpu.VMEM((n_tok, features), BF16),
-            pltpu.VMEM((2, n_tok), jnp.int32),
-            pltpu.VMEM((2, n_tok), BF16),
-            pltpu.VMEM((1, NX * NX), jnp.int32),
-            pltpu.VMEM((2, slots, features), BF16),
             pltpu.VMEM((2, slots, features), BF16),
             pltpu.VMEM((2, slots, hidden_units), F32),
             pltpu.VMEM((2, slots // 2, hidden_units), BF16),
@@ -448,7 +475,7 @@
             pltpu.VMEM((2, 2, slots // (2 * NZ), hidden_units), BF16),
             pltpu.VMEM((2, slots, hidden_units), BF16),
             pltpu.VMEM((2, slots, features), BF16),
-            dma((7,)),
+            dma((2,)),
             dma((2, 2)),
             dma((2,)),
             dma((n_chunks, 2)),
@@ -466,7 +493,7 @@
             dma((n_chunks, 2)),
             dma((2,)),
             dma((2,)),
-            dma((4,)),
+            dma((2,)),
             dma((n_chunks,)),
         ],
         compiler_params=pltpu.CompilerParams(
@@ -476,7 +503,7 @@
             flops=flops, bytes_accessed=4 * features * hidden_units, transcendentals=slots * hidden_units // 8
         ),
         name="moe_exchange",
-    )(tokens, cotangent, routes.T, route_weights.T, capacity_plan[None], up_weight, down_weight)
+    )(sent, up_weight, down_weight)
     return pl.pallas_call(
         combine_kernel,
         out_shape=(

time: 84 us -> 87.3 us (1.039)
  Pallas kernels: 83.1 us -> 84.8 us
  local copies, waits for them, and re-layouts: 0 us -> 1.5 us
    pallas_call x0 -> x1, Pallas kernels: none -> 2.83 us  [per_device(): pl.pallas_call(route_kernel, out_shape=(jax.ShapeDtypeStruct((2, slots, f...]
    unnamed x0 -> x6, local copies, waits for them, and re-layouts: none -> 1.5 us
    pallas_call x1, Pallas kernels: 7.68 us -> 6.49 us  [per_device(): pl.pallas_call(combine_kernel, out_shape=(jax.ShapeDtypeStruct((n_tok, fe...]
where the time goes in v8:
time: 87.3 us; the launch traced here: 87.1 us
  Pallas kernels  84.8 us (97%)
  local copies, waits for them, and re-layouts  1.5 us (2%)
    pallas_call x1, Pallas kernels, per_device(): pl.pallas_call(moe_kernel, out_shape=(jax.ShapeDtypeStruct((2, NX * NX, C...  75.5 us
    pallas_call x1, Pallas kernels, per_device(): pl.pallas_call(combine_kernel, out_shape=(jax.ShapeDtypeStruct((n_tok, fe...  6.49 us
    pallas_call x1, Pallas kernels, per_device(): pl.pallas_call(route_kernel, out_shape=(jax.ShapeDtypeStruct((2, slots, f...  2.83 us

profile of v8, /device:TPU:1, one launch (start us, length us, event | category | flops | bytes accessed | tf_op | source)
XLA Modules:
  0.0 87.1 jit_solution(12121119201709629066)
XLA Ops:
  0.6 2.8 %route.1 = (bf16[2,512,896]{2,1,0:T(8,128)(2,1)}, bf16[512,128]{1,0:T(8,128)(2,1)}, bf16[512,128]{1,0:T(8,128)(2,1)}) custom-call(bf16[128,896]{1,0:T(8,128)(2,1)} %tokens_hbm.1, bf16[128,896]{1,0:T(8,128)(2,1)} %cotangent_hbm.1, s32[2,128]{1,0:T(2,128)} %bitcast.3, bf16[2,128]{1,0:T(2,128)(2,1)} %bitcast.4, s32[1,16]{1,0:T(1,128)} %bitcast.5), custom_call_target="tpu_custom_call" | custom-call | flops 234881024 | bytes 2752512 | tf_op jit(solution)/shard_map/route/pallas_call | solution.py:427
  3.5 0.0 copy-start.2
  3.5 1.5 %copy-done.2 = bf16[2,512,896]{2,1,0:T(8,128)(2,1)S(1)} copy-done((bf16[2,512,896]{2,1,0:T(8,128)(2,1)S(1)}, bf16[2,512,896]{2,1,0:T(8,128)(2,1)}, u32[]{:S(2)}) %copy-start.2) | copy-done | bytes 1835032
  5.0 0.0 copy-start
  5.0 0.0 copy-start.1
  5.0 75.5 %moe_exchange.1 = (bf16[2,16,32,896]{3,2,1,0:T(8,128)(2,1)S(1)}, bf16[512,2432]{1,0:T(8,128)(2,1)S(1)}, bf16[896,512]{1,0:T(8,128)(2,1)S(1)}, bf16[1,2432,896]{2,1,0:T(8,128)(2,1)S(1)}) custom-call(bf16[2,512,896]{2,1,0:T(8,128)(2,1)S(1)} %copy-done.2, bf16[1,896,2432]{2,1,0:T(8,128)(2,1)} %up_hbm.1, bf16[1,2432,896]{2,1,0:T(8,128)(2,1)} %down_hbm.1), custom_call_target="tpu_custom_call" | custom-call | flops 13388218368 | bytes 8716288 | tf_op jit(solution)/shard_map/moe_exchange/pallas_call | solution.py:454
  80.4 0.0 copy-done
  80.5 0.0 copy-done.1
  80.5 6.5 %combine.1 = (bf16[128,896]{1,0:T(8,128)(2,1)}, bf16[128,896]{1,0:T(8,128)(2,1)}, bf16[1,896,2432]{2,1,0:T(8,128)(2,1)}, bf16[1,2432,896]{2,1,0:T(8,128)(2,1)}) custom-call(bf16[2,16,32,896]{3,2,1,0:T(8,128)(2,1)S(1)} %get-tuple-element.12.returned_hbm, bf16[512,128]{1,0:T(8,128)(2,1)S(1)} %copy-done, bf16[512,128]{1,0:T(8,128)(2,1)S(1)} %copy-done.1, ...), custom_call_target="tpu_custom_call" | custom-call | flops 234881024 | bytes 17432576 | tf_op jit(solution)/shard_map/combine/pallas_call | solution.py:507
Async XLA Ops:
  3.5 1.5 %copy-start.2 = (bf16[2,512,896]{2,1,0:T(8,128)(2,1)S(1)}, bf16[2,512,896]{2,1,0:T(8,128)(2,1)}, u32[]{:S(2)}) copy-start(bf16[2,512,896]{2,1,0:T(8,128)(2,1)} %get-tuple-element.11.sent) | copy-start | bytes 5505028
  5.0 75.5 %copy-start = (bf16[512,128]{1,0:T(8,128)(2,1)S(1)}, bf16[512,128]{1,0:T(8,128)(2,1)}, u32[]{:S(2)}) copy-start(bf16[512,128]{1,0:T(8,128)(2,1)} %get-tuple-element.13.placer_hbm) | copy-start | bytes 393220
  5.0 75.5 %copy-start.1 = (bf16[512,128]{1,0:T(8,128)(2,1)S(1)}, bf16[512,128]{1,0:T(8,128)(2,1)}, u32[]{:S(2)}) copy-start(bf16[512,128]{1,0:T(8,128)(2,1)} %get-tuple-element.14.weighted_hbm) | copy-start | bytes 393220

commit v9 on v7

--- a/solution.py
+++ b/solution.py
@@ -93,6 +93,10 @@
         remote(ref, ref, sem, sem, mate).wait_send()
 
     barrier = pltpu.get_barrier_semaphore()
+    for peer in sources[1:]:
+        pl.semaphore_signal(barrier, inc=1, device_id={"expert": peer, "tensor": place}, device_id_type=MESH)
+    for device in (next_chip, prev_chip, mate):
+        pl.semaphore_signal(barrier, inc=1, device_id=device, device_id_type=MESH)
     load_tokens = pltpu.make_async_copy(tokens_hbm, tokens, load_sem.at[2])
     load_cotangent = pltpu.make_async_copy(cotangent_hbm, cotangent, load_sem.at[3])
     load_up = pltpu.make_async_copy(up_hbm.at[0], up, load_sem.at[0])
@@ -105,10 +109,6 @@
     ]
     for load in (*load_routing, load_tokens):
         load.start()
-    for peer in sources[1:]:
-        pl.semaphore_signal(barrier, inc=1, device_id={"expert": peer, "tensor": place}, device_id_type=MESH)
-    for device in (next_chip, prev_chip, mate):
-        pl.semaphore_signal(barrier, inc=1, device_id=device, device_id_type=MESH)
 
     for load in load_routing:
         load.wait()
@@ -383,14 +383,11 @@
         pltpu.make_async_copy(up.at[:, lo:hi], up_grad.at[0, :, lo:hi], up_sem.at[index])
         for index, (lo, hi) in enumerate(tiles)
     ]
-    for load in (load_flipped, *load_slope[:2]):
+    for load in (load_flipped, load_slope[0], loads[0], *load_slope[1:], *loads[1:], *parts[0], *parts[1]):
         load.start()
     load_flipped.wait()
     for index, (lo, hi) in enumerate(tiles):
         load_slope[index].wait()
-        if index == 0:
-            for load in (loads[0], *load_slope[2:], *loads[1:], *parts[0], *parts[1]):
-                load.start()
         up[:, lo:hi] = jnp.dot(flipped[...], slope[:, lo:hi], preferred_element_type=F32).astype(BF16)
         up_stores[index].start()
         if index < PIECES:

time: 84 us -> 83.8 us (level)
  no operation moved by 1% of the time
where the time goes in v9:
time: 83.8 us; the launch traced here: 83.7 us
  Pallas kernels  82.9 us (99%)
    pallas_call x1, Pallas kernels, per_device(): pl.pallas_call(moe_kernel, out_shape=(jax.ShapeDtypeStruct((2, NX * NX, C...  75.4 us
    pallas_call x1, Pallas kernels, per_device(): pl.pallas_call(combine_kernel, out_shape=(jax.ShapeDtypeStruct((n_tok, fe...  7.49 us

profile of v9, /device:TPU:1, one launch (start us, length us, event | category | flops | bytes accessed | tf_op | source)
XLA Modules:
  0.0 83.7 jit_solution(17249666339553558634)
XLA Ops:
  0.6 75.4 %moe_exchange.1 = (bf16[2,16,32,896]{3,2,1,0:T(8,128)(2,1)}, bf16[512,2432]{1,0:T(8,128)(2,1)}, bf16[896,512]{1,0:T(8,128)(2,1)}, bf16[1,2432,896]{2,1,0:T(8,128...) custom-call(bf16[128,896]{1,0:T(8,128)(2,1)} %tokens_hbm.1, bf16[128,896]{1,0:T(8,128)(2,1)} %cotangent_hbm.1, ...), custom_call_target="tpu_custom_call" | custom-call | flops 13388218368 | bytes 8716288 | tf_op jit(solution)/shard_map/moe_exchange/pallas_call | solution.py:414
  76.0 7.5 %combine.1 = (bf16[128,896]{1,0:T(8,128)(2,1)}, bf16[128,896]{1,0:T(8,128)(2,1)}, bf16[1,896,2432]{2,1,0:T(8,128)(2,1)}, bf16[1,2432,896]{2,1,0:T(8,128)(2,1)}) custom-call(bf16[2,16,32,896]{3,2,1,0:T(8,128)(2,1)} %get-tuple-element.10.returned_hbm, bf16[512,128]{1,0:T(8,128)(2,1)} %get-tuple-element.11.placer_hbm, ...), custom_call_target="tpu_custom_call" | custom-call | flops 234881024 | bytes 17432576 | tf_op jit(solution)/shard_map/combine/pallas_call | solution.py:477

commit v10 on v7

--- a/solution.py
+++ b/solution.py
@@ -21,11 +21,11 @@
 )
 CHUNKS = ((0, 4), (4, 8), (8, 12), (12, 16))
 ORDER = (
-    "P10", "P11", "P00", "P01", "A10", "A11", "P20", "B11", "B10", "A00", "P21", "C11",
-    "A01", "B00", "C10", "B01", "A20", "C00", "P30", "B20", "D10", "A21", "D00", "P31",
-    "C01", "C20", "D11", "E00", "E10", "B21", "D01", "A30", "F10", "D20", "A31", "F00",
-    "B30", "E01", "B31", "G10", "C30", "E20", "E11", "C31", "G00", "F01", "D30", "F20",
-    "C21", "F11", "G01", "D31", "G11", "E30", "D21", "G20", "E31", "X00", "F30", "G30",
+    "P10", "P11", "P00", "P01", "A10", "A11", "P20", "B11", "B10", "A00", "A01", "B00",
+    "P21", "A20", "C11", "C10", "B01", "C00", "P30", "B20", "D10", "A21", "D00", "P31",
+    "C01", "C20", "D11", "E00", "E10", "B21", "A30", "D01", "F10", "D20", "A31", "F00",
+    "B30", "E01", "B31", "G10", "C30", "E20", "E11", "C31", "G00", "F01", "D30", "C21",
+    "F20", "F11", "G01", "D31", "G11", "E30", "D21", "G20", "E31", "X00", "F30", "G30",
     "F31", "E21", "G31", "F21", "G21", "Y00",
 )
 TILE = 512
@@ -221,41 +221,37 @@
     def chip_sum(c, k, which, half):
         return part[k, block(c, core, which), half] + core_in[k, half_block(c, which), half].astype(F32)
 
-    def send_second(c, k, side, half):
-        remote(
-            second_out.at[k, side, small_block(c), half], second_in.at[k, side, small_block(c), half],
-            second_send.at[0], second_recv.at[c, k], next_chip if side == 0 else prev_chip,
-        ).start()
-
     def stage_core(c, k):
         await_received(core_in.at[k, half_block(c, 0, NZ)], core_recv.at[c, k])
         here = small_block(c)
-        for half in (half_a, half_b):
-            first_out[k, here, half] = chip_sum(c, k, z_far, half).astype(BF16)
-        second_out[k, 0, here, half_b] = chip_sum(c, k, z_next, half_b).astype(BF16)
-        second_out[k, 1, here, half_a] = chip_sum(c, k, z_prev, half_a).astype(BF16)
-        for half, device in ((half_a, next_chip), (half_b, prev_chip)):
+        for side, (for_a, for_b) in enumerate(((z_far, z_next), (z_prev, z_far))):
+            first_out[k, side, here, half_a] = chip_sum(c, k, for_a, half_a).astype(BF16)
+            first_out[k, side, here, half_b] = chip_sum(c, k, for_b, half_b).astype(BF16)
+        for side, device in ((0, next_chip), (1, prev_chip)):
             remote(
-                first_out.at[k, here, half], first_in.at[k, here, half], first_send.at[0], first_recv.at[c, k], device
+                first_out.at[k, side, here], first_in.at[k, side, here], first_send.at[0], first_recv.at[c, k], device
             ).start()
-        send_second(c, k, 0, half_b)
-        send_second(c, k, 1, half_a)
 
     def stage_relay(c, k):
         here = small_block(c)
-        relays = ((0, z_next, half_a), (1, z_prev, half_b))
-        await_received(first_in.at[k, here], first_recv.at[c, k])
-        for side, which, half in relays:
-            total = chip_sum(c, k, which, half) + first_in[k, here, half].astype(F32)
-            second_out[k, side, here, half] = total.astype(BF16)
-        for side, which, half in relays:
-            send_second(c, k, side, half)
+        relays = ((0, z_next, half_a, next_chip), (1, z_prev, half_b, prev_chip))
+        await_received(first_in.at[k, :, here], first_recv.at[c, k])
+        for side, which, half, device in relays:
+            total = chip_sum(c, k, which, half) + first_in[k, side, here, half].astype(F32)
+            second_out[k, here, half] = total.astype(BF16)
+        for side, which, half, device in relays:
+            remote(
+                second_out.at[k, here, half], second_in.at[k, here, half], second_send.at[0], second_recv.at[c, k],
+                device,
+            ).start()
 
     def stage_activate(c, k):
         here = small_block(c)
-        await_received(second_in.at[k, :, here], second_recv.at[c, k])
-        total = chip_sum(c, k, z, pl.ds(0, hidden_units))
-        total = total + (second_in[k, 0, here, :].astype(F32) + second_in[k, 1, here, :].astype(F32))
+        await_received(second_in.at[k, here], second_recv.at[c, k])
+        total = chip_sum(c, k, z, pl.ds(0, hidden_units)) + second_in[k, here, :].astype(F32)
+        total = total + jnp.concatenate(
+            [first_in[k, 1, here, half_a].astype(F32), first_in[k, 0, here, half_b].astype(F32)], axis=1
+        )
         mine = block(c, core, z)
         if k == 0:
             part[0, mine, :] = total
@@ -442,10 +438,10 @@
             pltpu.VMEM((2, slots, hidden_units), F32),
             pltpu.VMEM((2, slots // 2, hidden_units), BF16),
             pltpu.VMEM((2, slots // 2, hidden_units), BF16),
+            pltpu.VMEM((2, 2, slots // (2 * NZ), hidden_units), BF16),
+            pltpu.VMEM((2, 2, slots // (2 * NZ), hidden_units), BF16),
             pltpu.VMEM((2, slots // (2 * NZ), hidden_units), BF16),
             pltpu.VMEM((2, slots // (2 * NZ), hidden_units), BF16),
-            pltpu.VMEM((2, 2, slots // (2 * NZ), hidden_units), BF16),
-            pltpu.VMEM((2, 2, slots // (2 * NZ), hidden_units), BF16),
             pltpu.VMEM((2, slots, hidden_units), BF16),
             pltpu.VMEM((2, slots, features), BF16),
             dma((7,)),

time: 84 us -> 87.4 us (1.040)
  Pallas kernels: 83.1 us -> 86.4 us
    pallas_call x1, Pallas kernels: 75.4 us -> 78.8 us  [per_device(): pl.pallas_call(moe_kernel, out_shape=(jax.ShapeDtypeStruct((2, NX * NX, C...]
where the time goes in v10:
time: 87.4 us; the launch traced here: 87.2 us
  Pallas kernels  86.4 us (99%)
    pallas_call x1, Pallas kernels, per_device(): pl.pallas_call(moe_kernel, out_shape=(jax.ShapeDtypeStruct((2, NX * NX, C...  78.8 us
    pallas_call x1, Pallas kernels, per_device(): pl.pallas_call(combine_kernel, out_shape=(jax.ShapeDtypeStruct((n_tok, fe...  7.68 us

profile of v10, /device:TPU:1, one launch (start us, length us, event | category | flops | bytes accessed | tf_op | source)
XLA Modules:
  0.0 87.2 jit_solution(5883603221560032858)
XLA Ops:
  0.6 78.8 %moe_exchange.1 = (bf16[2,16,32,896]{3,2,1,0:T(8,128)(2,1)}, bf16[512,2432]{1,0:T(8,128)(2,1)}, bf16[896,512]{1,0:T(8,128)(2,1)}, bf16[1,2432,896]{2,1,0:T(8,128...) custom-call(bf16[128,896]{1,0:T(8,128)(2,1)} %tokens_hbm.1, bf16[128,896]{1,0:T(8,128)(2,1)} %cotangent_hbm.1, ...), custom_call_target="tpu_custom_call" | custom-call | flops 13388218368 | bytes 8716288 | tf_op jit(solution)/shard_map/moe_exchange/pallas_call | solution.py:413
  79.4 7.7 %combine.1 = (bf16[128,896]{1,0:T(8,128)(2,1)}, bf16[128,896]{1,0:T(8,128)(2,1)}, bf16[1,896,2432]{2,1,0:T(8,128)(2,1)}, bf16[1,2432,896]{2,1,0:T(8,128)(2,1)}) custom-call(bf16[2,16,32,896]{3,2,1,0:T(8,128)(2,1)} %get-tuple-element.10.returned_hbm, bf16[512,128]{1,0:T(8,128)(2,1)} %get-tuple-element.11.placer_hbm, ...), custom_call_target="tpu_custom_call" | custom-call | flops 234881024 | bytes 17432576 | tf_op jit(solution)/shard_map/combine/pallas_call | solution.py:476
